TPU v7x, 128 devices: a whole 4x4x4 slice. The times are simulated.
128 devices in a mesh: lat: 8 (over x, y_lo), lon: 16 (over y_hi, z, core).
Axes of the slice: x: 4, y: 4 (y_hi: 2, y_lo: 2; y = y_hi * 2 + y_lo), z: 4, core: 2. Of those that a mesh axis runs over, the one named last changes fastest.
Arguments:
- tokens: bfloat16 [2, 192, 192, 512], P(None, 'lat', 'lon'), may hold values from -6 to 6
- mask_ids: int32 [2, 192, 192], P(None, 'lat', 'lon'), may hold values from 0 to 8, as said below
- fine_bias: float32 [8, 144, 144], replicated, may hold values from -4 to 300
- fine_qkv: bfloat16 [512, 1536], replicated, may hold values from -0.25 to 0.25
- fine_out: bfloat16 [512, 512], replicated, may hold values from -0.25 to 0.25
- merge_weight: bfloat16 [2048, 1024], replicated, may hold values from -0.125 to 0.125
- coarse_bias: float32 [16, 144, 144], replicated, may hold values from -4 to 300
- coarse_qkv: bfloat16 [1024, 3072], replicated, may hold values from -0.1875 to 0.1875
- coarse_out: bfloat16 [1024, 1024], replicated, may hold values from -0.1875 to 0.1875
- cotangent: bfloat16 [2, 96, 96, 1024], P(None, 'lat', 'lon'), may hold values from -6 to 6
Outputs:
- coarse_result: bfloat16 [2, 96, 96, 1024], P(None, 'lat', 'lon')
- token_grad: bfloat16 [2, 192, 192, 512], P(None, 'lat', 'lon')
Inputs may be any that keep to these rules, and one draw needn't show every extreme that they name: mask_ids = 3 * level region + latitude region of the shifted grid: the level region is 0 below level 0, 1 below 1, else 2; the latitude region is 0 below row 186, 2 in the last r rows, else 1, where r, from 1 to 5, is drawn separately for each level and each longitude column.
All inputs are finite; a program needn't handle non-finite values.
Results may differ from a plain program's by a relative error of at most 0.022.
Values may be sent and summed in bfloat16 or wider, within the bound.
A program may use at most 128 MiB of HBM per device.

v0:
```python
import functools

import jax
import jax.numpy as jnp
import numpy as np
from jax import lax
from jax.experimental import pallas as pl
from jax.experimental.pallas import tpu as pltpu
from jax.sharding import PartitionSpec as P

F32 = jnp.float32
BF16 = jnp.bfloat16
EPSILON = 1e-05
MASKED = -1e30
MESH = pl.DeviceIdType.MESH

UNIT = 80
PART = 176
QUARTER = 96
NEIGHBOURS = [(a, b) for a in (-1, 0, 1) for b in (-1, 0, 1) if (a, b) != (0, 0)] + [(0, 2), (0, -2)]


def one_hot(pairs, rows, columns):
    out = np.zeros((rows, columns), np.float32)
    for r, c in pairs:
        out[r, c] = 1.0
    return out


def region_of(row, col):
    if row >= 3:
        return (row - 3) * 6 + col - 6 if col >= 6 else 128 + (row - 3) * 6 + col
    return 256 + row * 6 + col - 6 if col >= 6 else 288 + row * 6 + col


def part_of(s, o):
    half, c = divmod(o, 6)
    if s < 9:
        at = s * 6 + c
    elif s < 21:
        at = 64 + (s - 9) * 6 + c
    else:
        at = 144 + (s - 21) * 6 + c
    return half * PART + at


@functools.cache
def row_orders():
    to_region = one_hot([(region_of(r, c), r * 16 + c) for r in range(24) for c in range(12)], 320, 384)
    unit_pairs, part_pairs = [], []
    for s in range(24):
        for o in range(12):
            unit = UNIT * (s // 6) + 12 * (s % 6) + o
            unit_pairs.append((unit, region_of((s + 3) % 24, (o + 6) % 12)))
            part_pairs.append((part_of(s, o), unit))
    to_unit = one_hot(unit_pairs, 320, 320)
    to_part = one_hot(part_pairs, 2 * PART, 320)
    merge = np.zeros((2, 4, 72, 4 * QUARTER), np.float32)
    for u in range(2):
        for k, (dr, dc) in enumerate([(0, 0), (1, 0), (0, 1), (1, 1)]):
            for r in range(6):
                for c in range(12):
                    quarter, col = divmod(2 * c + dc, 6)
                    s = 12 * u + 2 * r + dr - 3
                    if u == 1:
                        at = (s - 9) * 6 + col
                    else:
                        at = 64 + (s + 3) * 6 + col if s < 0 else s * 6 + col
                    merge[u, k, r * 12 + c, quarter * QUARTER + at] = 1.0
    coarse = one_hot(
        [
            (l * 72 + r * 12 + c, (((c // 6) * 2 + l) * 6 + r) * 16 + c % 6)
            for l in range(2)
            for r in range(6)
            for c in range(12)
        ],
        144,
        384,
    )
    id_row = one_hot([(t, t // 12 + 2) for t in range(72)], UNIT, 8)
    id_col = one_hot([(t, t % 12) for t in range(72)], UNIT, 12)
    both = lambda m: [m, np.swapaxes(m, -1, -2)]
    orders = both(to_region) + both(to_unit) + both(to_part) + both(merge) + both(coarse)
    return [np.ascontiguousarray(m).astype(jnp.bfloat16) for m in orders] + [id_row, id_col]


def dot(a, b):
    return lax.dot_general(a, b, (((1,), (0,)), ((), ())), preferred_element_type=F32)


def dot_nt(a, b):
    return lax.dot_general(a, b, (((1,), (1,)), ((), ())), preferred_element_type=F32)


def dot_tn(a, b):
    return lax.dot_general(a, b, (((0,), (0,)), ((), ())), preferred_element_type=F32)


def normed_rows(x):
    center = x - jnp.mean(x, axis=-1, keepdims=True)
    scale = lax.rsqrt(jnp.mean(center * center, axis=-1, keepdims=True) + EPSILON)
    return center * scale, scale


def norm_grad(grad, hat, scale):
    inner = jnp.mean(grad * hat, axis=-1, keepdims=True)
    return scale * (grad - jnp.mean(grad, axis=-1, keepdims=True) - hat * inner)


def one_row(x):
    span = x.shape[0] // 2
    low = lax.broadcasted_iota(jnp.int32, (span, 128), 1) < 64
    return jnp.where(low, x[:span], x[span:])


def rows_at(start, size, unit=16):
    return pl.ds(pl.multiple_of(start, unit), size)


def loop(count, body):
    lax.fori_loop(0, count, lambda t, c: (body(t), c)[1], 0)


class Box:
    def __init__(self, **fields):
        self.__dict__.update(fields)


ARGS = dict(
    tokens=0, mask_ids=1, fine_bias=0, fine_qkv=0, fine_out=0, merge_weight=0, coarse_bias=0, coarse_qkv=0,
    coarse_out=0, cotangent=2, to_region=0, to_region_t=0, to_unit=0, to_unit_t=0, to_part=0, to_part_t=0,
    merge=0, merge_t=0, coarse=0, coarse_t=0, id_row=1, id_col=1,
)
LOADED = dict(
    tokens=0, to_region=0, to_unit=0, fine_bias=0, fine_qkv=0, fine_out=0, to_part=0, coarse=0, coarse_bias=0,
    merge=1, merge_weight=0, coarse_qkv=0, coarse_out=0, coarse_t=0, merge_t=1, to_part_t=0, to_unit_t=0,
    to_region_t=0,
)
SCRATCH = dict(
    x16=((2, 24, 16, 512), BF16),
    heads2=((160, 128), BF16),
    heads2_c=((288, 128), BF16),
    send1=((2, 192, 512), BF16),
    region=((2, 320, 512), BF16),
    unit_x=((640, 512), BF16),
    unit_n=((640, 512), BF16),
    hat_f=((640, 512), F32),
    scale_f=((640, 128), F32),
    proj=((704, 1536), BF16),
    bias_f=((2, 2, 4, 160, 128), F32),
    raised_f=((8, 4, 160, 128), BF16),
    recip_f=((640, 512), F32),
    heads_f=((640, 512), BF16),
    send2=((2, 2, PART, 512), BF16),
    quarters=((2, 4, QUARTER, 512), BF16),
    hat_m=((144, 2048), F32),
    scale_m=((144, 128), F32),
    normed_m=((144, 2048), BF16),
    merged=((144, 1024), BF16),
    hat_c=((144, 1024), F32),
    scale_c=((144, 128), F32),
    normed_c=((144, 1024), BF16),
    proj_c=((256, 3072), BF16),
    bias_c=((16, 144, 256), F32),
    raised_c=((8, 288, 256), BF16),
    recip_c=((144, 1024), F32),
    heads_c=((144, 1024), BF16),
    result=((144, 1024), BF16),
    result16=((2, 2, 6, 6, 1024), BF16),
    cot_raw=((2, 2, 6, 6, 1024), BF16),
    cot16=((2, 2, 6, 16, 1024), BF16),
    cot=((144, 1024), BF16),
    dheads_c=((144, 1024), BF16),
    dprod_c=((144, 1024), BF16),
    dproj_c=((144, 3072), BF16),
    grad_c=((144, 1024), F32),
    dmerged=((144, 1024), BF16),
    grad_m=((144, 2048), F32),
    send3=((2, 4, QUARTER, 512), BF16),
    part=((2, 2, PART, 512), BF16),
    dmixed=((640, 512), BF16),
    dheads_f=((640, 512), BF16),
    dprod_f=((640, 512), BF16),
    dproj_f=((640, 1536), BF16),
    send4=((2, 192, 512), BF16),
    region4=((2, 320, 512), BF16),
)
def kernel(n_lat, n_lon, *refs):
    rest = list(refs)
    hbm = Box(**{name: rest.pop(0) for name in ARGS})
    result_ref, grad_ref = rest.pop(0), rest.pop(0)
    vm = Box(**{name: rest.pop(0) for name in SCRATCH})
    ld = Box(**{name: rest.pop(0) for name in LOADED})
    load_sem, send_sem, recv_sem, near_sem = rest

    i, j = lax.axis_index("lat"), lax.axis_index("lon")
    odd = lax.rem(j, 2)
    even = odd == 0

    def device(di, dj):
        return (lax.rem(i + di + n_lat, n_lat), lax.rem(j + dj + n_lon, n_lon))

    def remote(src, dst, sem, l, target):
        return pltpu.make_async_remote_copy(
            src_ref=src,
            dst_ref=dst,
            send_sem=send_sem.at[sem, l],
            recv_sem=recv_sem.at[sem, l],
            device_id=target,
            device_id_type=MESH,
        )

    vm.quarters[:, :, 80:, :] = jnp.zeros((2, 4, QUARTER - 80, 512), BF16)
    barrier = pltpu.get_barrier_semaphore()
    for di, dj in NEIGHBOURS:
        pl.semaphore_signal(barrier, inc=1, device_id=device(di, dj), device_id_type=MESH)

    loads = Box()
    for at, (name, paired) in enumerate(LOADED.items()):
        src = getattr(hbm, name)
        if paired:
            src = src.at[odd]
        copy = pltpu.make_async_copy(src, getattr(ld, name), load_sem.at[at])
        copy.start()
        setattr(loads, name, copy)
    own_cot = pltpu.make_async_copy(
        hbm.cotangent.at[:, pl.ds(6 * odd, 6)], vm.cot_raw.at[odd], near_sem.at[0, 0]
    )
    own_cot.start()

    vm.x16[:, :, 12:, :] = jnp.zeros((2, 24, 4, 512), BF16)
    vm.cot16[:, :, :, 6:, :] = jnp.zeros((2, 2, 6, 10, 1024), BF16)
    for end in (320, 640):
        vm.proj[end : end + 64, :] = jnp.zeros((64, 1536), BF16)
    vm.proj_c[144:, :] = jnp.zeros((112, 3072), BF16)
    for ref in (vm.heads2, vm.heads2_c):
        low = lax.broadcasted_iota(jnp.int32, ref.shape, 1) < 64
        first = lax.broadcasted_iota(jnp.int32, ref.shape, 0) < ref.shape[0] // 2
        ref[...] = jnp.where(low == first, 1.0, 0.0).astype(BF16)

    def two_heads(x, mask):
        return jnp.concatenate([x, x], axis=0) * mask[...]

    loads.tokens.wait()
    loads.to_region.wait()
    vm.x16[:, :, :12, :] = ld.tokens[...]
    pl.semaphore_wait(barrier, len(NEIGHBOURS))
    pieces = [(0, 128, (0, -1)), (128, 32, (-1, 0)), (160, 32, (-1, -1))]

    def first(l):
        return [
            remote(
                vm.send1.at[l, pl.ds(at, size)], vm.region.at[l, pl.ds(128 + at, size)], n, l, device(*to)
            )
            for n, (at, size, to) in enumerate(pieces)
        ]

    def regions(l):
        ordered = dot(ld.to_region[...], vm.x16[l].reshape(384, 512)).astype(BF16)
        vm.region[l, :128, :] = ordered[:128]
        vm.send1[l] = ordered[128:]
        for copy in first(l):
            copy.start()

    loop(2, regions)
    partner_cot = remote(
        hbm.cotangent.at[:, pl.ds(6 - 6 * odd, 6)], vm.cot_raw.at[odd], 3, 0, device(0, 1 - 2 * odd)
    )
    partner_cot.start()

    loads.fine_bias.wait()
    lanes = lax.broadcasted_iota(jnp.int32, (UNIT, 128), 1)
    subs = lax.broadcasted_iota(jnp.int32, (UNIT, 128), 0)
    past = jnp.where(lanes >= 72, MASKED, 0.0).astype(F32)
    for level in range(2):
        spread = dot(hbm.id_row[...], hbm.mask_ids[level, 16:24, :].astype(F32))
        id_of = jnp.sum(spread * hbm.id_col[...], axis=-1, keepdims=True)
        id_at = dot(jnp.ones((8, UNIT), F32), jnp.where(lanes == subs, id_of, 0.0))[:1]
        apart = jnp.where(id_of == id_at, past, MASKED)
        for head in range(8):
            span = slice(72 * level, 72 * level + 72)
            block = ld.fine_bias[head, span, span]
            block = jnp.concatenate([block, jnp.zeros((72, 56), F32)], axis=1)
            block = jnp.concatenate([block, jnp.zeros((8, 128), F32)], axis=0)
            at = slice(UNIT * (head % 2), UNIT * (head % 2) + UNIT)
            vm.bias_f[0, level, head // 2, at, :] = block + past
            vm.bias_f[1, level, head // 2, at, :] = block + apart

    loads.coarse_bias.wait()

    def coarse_pad(h):
        vm.bias_c[h] = jnp.concatenate([ld.coarse_bias[h], jnp.full((144, 112), MASKED, F32)], axis=1)

    loop(16, coarse_pad)
    loads.to_unit.wait()
    loads.fine_qkv.wait()
    loads.fine_out.wait()
    loads.to_part.wait()

    own, next_, before = (0, 64, 0), (64, 80, 0), (144, 32, 64)

    def second(l, kind, half, sem, q, to):
        at, size, into = kind
        return remote(
            vm.send2.at[l, half, pl.ds(at, size)], vm.quarters.at[l, q, pl.ds(into, size)], sem, l, device(*to)
        )

    def second_near(l, kind, half, sem, q):
        at, size, into = kind
        return pltpu.make_async_copy(
            vm.send2.at[l, half, pl.ds(at, size)], vm.quarters.at[l, q, pl.ds(into, size)], near_sem.at[sem, l]
        )

    side = (0, 1)
    even_sends = [
        (next_, 0, 5, 1, (0, 1)), (next_, 1, 6, 2, (0, 1)), (before, 0, 9, 1, (1, 0)), (before, 1, 10, 2, (1, 0)),
    ]
    even_near = [(own, 0, 1, 1), (own, 1, 2, 2)]
    even_takes = [
        (own, 0, 4, 0, side), (own, 0, 7, 3, side), (before, 0, 8, 0, side), (before, 0, 9, 1, side),
        (before, 0, 10, 2, side), (before, 0, 11, 3, side),
    ]
    odd_sends = [
        (own, 1, 4, 0, (0, 1)), (next_, 1, 12, 0, (0, 2)), (before, 1, 8, 0, (1, 1)), (own, 0, 7, 3, (0, -1)),
        (before, 0, 11, 3, (1, -1)),
    ]
    odd_near = [(next_, 0, 1, 3)]
    odd_takes = [(next_, 0, 12, 0, side), (next_, 0, 5, 1, side), (next_, 0, 6, 2, side)]

    def by_parity(of_even, of_odd):
        @pl.when(even)
        def _():
            of_even()

        @pl.when(odd == 1)
        def _():
            of_odd()

    def start_all(far, near, far_list, near_list, l):
        for args in far_list:
            far(l, *args).start()
        for args in near_list:
            near(l, *args).start()

    def take_all(far, near, take_list, near_list, l):
        for args in near_list:
            near(l, *args).wait()
        for args in take_list:
            far(l, *args).wait_recv()

    def sent_all(far, far_list, l):
        for args in far_list:
            far(l, *args).wait_send()

    def fine_forward(l):
        base = l * 320
        level = rows_at(base, 320)
        for copy in first(l):
            copy.wait()
        vm.unit_x[level, :] = dot(ld.to_unit[...], vm.region[l]).astype(BF16)

        def fine_norm(t):
            at = rows_at(base + t * 80, 80)
            hat, scale = normed_rows(vm.unit_x[at, :].astype(F32))
            vm.hat_f[at, :] = hat
            vm.scale_f[at, :] = jnp.broadcast_to(scale, (80, 128))
            vm.unit_n[at, :] = hat.astype(BF16)

        loop(4, fine_norm)

        def fine_project(t):
            cols = rows_at(t * 512, 512, 512)
            scale = jnp.where(t < 1, 0.125, 1.0).astype(F32)
            vm.proj[level, cols] = (dot(vm.unit_n[level, :], ld.fine_qkv[:, cols]) * scale).astype(BF16)

        loop(3, fine_project)

        def fine_attend(m):
            last = lax.div(m, 3)
            at, wide = rows_at(base + m * UNIT, UNIT), rows_at(base + m * UNIT, 128)
            pairs = [slice(128 * p, 128 * p + 128) for p in range(4)]
            ones = jnp.ones((128, 128), BF16)
            scores = [
                dot_nt(two_heads(vm.proj[at, pair], vm.heads2), vm.proj[wide, 512 + pair.start : 512 + pair.stop])
                + vm.bias_f[last, 1 - l, p]
                for p, pair in enumerate(pairs)
            ]
            tops = [jnp.max(s, axis=-1, keepdims=True) for s in scores]
            raised = [jnp.exp(s - t).astype(BF16) for s, t in zip(scores, tops)]
            sums = [
                dot(e, jnp.concatenate([vm.proj[wide, 1024 + pair.start : 1024 + pair.stop], ones], axis=1))
                for e, pair in zip(raised, pairs)
            ]
            for p, pair in enumerate(pairs):
                recip = 1.0 / one_row(sums[p][:, 128:])
                vm.raised_f[l * 4 + m, p] = raised[p]
                vm.recip_f[at, pair] = recip
                vm.heads_f[at, pair] = (one_row(sums[p][:, :128]) * recip).astype(BF16)

        loop(4, fine_attend)
        mixed = vm.unit_x[level, :].astype(F32) + dot(vm.heads_f[level, :], ld.fine_out[...])
        ordered = dot(ld.to_part[...], mixed.astype(BF16))
        vm.send2[l] = ordered.astype(BF16).reshape(2, PART, 512)
        by_parity(
            lambda: start_all(second, second_near, even_sends, even_near, l),
            lambda: start_all(second, second_near, odd_sends, odd_near, l),
        )

    loop(2, fine_forward)

    own_cot.wait()
    partner_cot.wait()
    loads.coarse.wait()
    vm.cot16[:, :, :, :6, :] = vm.cot_raw[...]
    vm.cot[...] = dot(ld.coarse[...], vm.cot16[...].reshape(384, 1024)).astype(BF16)
    loads.coarse_out.wait()
    loads.merge.wait()
    loads.merge_weight.wait()
    loads.coarse_qkv.wait()
    loads.coarse_t.wait()

    def coarse_cot(t):
        cols = rows_at(t * 512, 512, 512)
        vm.grad_c[:, cols] = dot_nt(vm.cot[...], ld.coarse_out[cols, :])

    loop(2, coarse_cot)

    def gather(l):
        by_parity(
            lambda: take_all(second, second_near, even_takes, even_near, l),
            lambda: take_all(second, second_near, odd_takes, odd_near, l),
        )
        source = vm.quarters[l].reshape(4 * QUARTER, 512)
        for k in range(4):
            vm.hat_m[rows_at(l * 72, 72, 8), 512 * k : 512 * k + 512] = dot(ld.merge[k], source)

    loop(2, gather)

    def merge_norm(t):
        at = rows_at(t * 48, 48)
        hat, scale = normed_rows(vm.hat_m[at, :])
        vm.hat_m[at, :] = hat
        vm.scale_m[at, :] = jnp.broadcast_to(scale, (48, 128))
        vm.normed_m[at, :] = hat.astype(BF16)

    loop(3, merge_norm)

    def merge_project(t):
        cols = rows_at(t * 512, 512, 512)
        vm.merged[:, cols] = dot(vm.normed_m[...], ld.merge_weight[:, cols]).astype(BF16)

    loop(2, merge_project)

    def coarse_norm(t):
        at = rows_at(t * 48, 48)
        hat, scale = normed_rows(vm.merged[at, :].astype(F32))
        vm.hat_c[at, :] = hat
        vm.scale_c[at, :] = jnp.broadcast_to(scale, (48, 128))
        vm.normed_c[at, :] = hat.astype(BF16)

    loop(3, coarse_norm)

    def coarse_project(t):
        cols = rows_at(t * 512, 512, 512)
        scale = jnp.where(t < 2, 0.125, 1.0).astype(F32)
        vm.proj_c[:144, cols] = (dot(vm.normed_c[...], ld.coarse_qkv[:, cols]) * scale).astype(BF16)

    loop(6, coarse_project)

    def cols_at(p, base):
        return rows_at(p * 128 + base, 128, 128)

    def coarse_attend(t):
        pairs = [2 * t, 2 * t + 1]
        ones = jnp.ones((256, 128), BF16)
        scores = [
            dot_nt(two_heads(vm.proj_c[:144, cols_at(p, 0)], vm.heads2_c), vm.proj_c[:, cols_at(p, 1024)])
            + vm.bias_c[pl.ds(2 * p, 2)].reshape(288, 256)
            for p in pairs
        ]
        tops = [jnp.max(s, axis=-1, keepdims=True) for s in scores]
        raised = [jnp.exp(s - top).astype(BF16) for s, top in zip(scores, tops)]
        sums = [
            dot(e, jnp.concatenate([vm.proj_c[:, cols_at(p, 2048)], ones], axis=1))
            for e, p in zip(raised, pairs)
        ]
        for p, e, total in zip(pairs, raised, sums):
            recip = 1.0 / one_row(total[:, 128:])
            vm.raised_c[p] = e
            vm.recip_c[:, cols_at(p, 0)] = recip
            vm.heads_c[:, cols_at(p, 0)] = (one_row(total[:, :128]) * recip).astype(BF16)

    loop(4, coarse_attend)

    def coarse_mix(t):
        cols = rows_at(t * 512, 512, 512)
        mixed = dot(vm.heads_c[...], ld.coarse_out[:, cols])
        vm.result[:, cols] = (vm.merged[:, cols].astype(F32) + mixed).astype(BF16)
        grad = vm.grad_c[:, cols] * vm.recip_c[:, cols]
        vm.dheads_c[:, cols] = grad.astype(BF16)
        vm.dprod_c[:, cols] = (grad * vm.heads_c[:, cols].astype(F32)).astype(BF16)

    loop(2, coarse_mix)

    def spread_result(h):
        rows = dot(ld.coarse_t[rows_at(h * 192, 192), :], vm.result[...]).astype(BF16)
        vm.result16[h] = rows.reshape(2, 6, 16, 1024)[:, :, :6]

    loop(2, spread_result)
    into = result_ref.at[:, pl.ds(6 * odd, 6)]
    result_near = pltpu.make_async_copy(vm.result16.at[odd], into, near_sem.at[3, 0])
    result_far = remote(vm.result16.at[1 - odd], into, 13, 0, device(0, 1 - 2 * odd))
    result_near.start()
    result_far.start()

    def coarse_attend_grad(t):
        pairs = [2 * t, 2 * t + 1]
        minus = jnp.full((256, 128), -1.0, BF16)
        grads = [two_heads(vm.dheads_c[:, cols_at(p, 0)], vm.heads2_c) for p in pairs]
        prods = [two_heads(vm.dprod_c[:, cols_at(p, 0)], vm.heads2_c) for p in pairs]
        queries = [two_heads(vm.proj_c[:144, cols_at(p, 0)], vm.heads2_c) for p in pairs]
        inner = [
            dot_nt(
                jnp.concatenate([g, d], axis=1), jnp.concatenate([vm.proj_c[:, cols_at(p, 2048)], minus], axis=1)
            )
            for p, g, d in zip(pairs, grads, prods)
        ]
        dscores = [(vm.raised_c[p].astype(F32) * x).astype(BF16) for p, x in zip(pairs, inner)]
        for p, g, q, ds in zip(pairs, grads, queries, dscores):
            vm.dproj_c[:, cols_at(p, 2048)] = dot_tn(vm.raised_c[p], g)[:144].astype(BF16)
            dq = one_row(dot(ds, vm.proj_c[:, cols_at(p, 1024)]))
            vm.dproj_c[:, cols_at(p, 0)] = (dq * 0.125).astype(BF16)
            vm.dproj_c[:, cols_at(p, 1024)] = dot_tn(ds, q)[:144].astype(BF16)

    loop(4, coarse_attend_grad)

    def coarse_project_grad(t):
        cols = rows_at(t * 512, 512, 512)
        vm.grad_c[:, cols] = dot_nt(vm.dproj_c[...], ld.coarse_qkv[cols, :])

    loop(2, coarse_project_grad)

    def coarse_norm_grad(t):
        at = rows_at(t * 48, 48)
        grad = norm_grad(vm.grad_c[at, :], vm.hat_c[at, :], vm.scale_c[at, :1])
        vm.dmerged[at, :] = (vm.cot[at, :].astype(F32) + grad).astype(BF16)

    loop(3, coarse_norm_grad)

    def merge_project_grad(t):
        cols = rows_at(t * 512, 512, 512)
        vm.grad_m[:, cols] = dot_nt(vm.dmerged[...], ld.merge_weight[cols, :])

    loop(4, merge_project_grad)
    loads.merge_t.wait()

    def third(l, kind, half, sem, q, to):
        at, size, into = kind
        return remote(
            vm.send3.at[l, q, pl.ds(into, size)], vm.part.at[l, half, pl.ds(at, size)], sem, l, device(*to)
        )

    def third_near(l, kind, half, sem, q):
        at, size, into = kind
        return pltpu.make_async_copy(
            vm.send3.at[l, q, pl.ds(into, size)], vm.part.at[l, half, pl.ds(at, size)], near_sem.at[sem, l]
        )

    even_back = [
        (own, 1, 15, 0, (0, -1)), (own, 0, 14, 3, (0, 1)), (before, 1, 19, 0, (-1, -1)),
        (before, 0, 18, 1, (-1, 0)), (before, 1, 20, 2, (-1, 0)), (before, 0, 21, 3, (-1, 1)),
    ]
    even_back_near = [(own, 0, 4, 1), (own, 1, 5, 2)]
    even_back_takes = [
        (next_, 0, 16, 0, side), (next_, 1, 17, 0, side), (before, 0, 18, 0, side), (before, 1, 20, 0, side),
    ]
    odd_back = [(next_, 1, 22, 0, (0, -2)), (next_, 0, 16, 1, (0, -1)), (next_, 1, 17, 2, (0, -1))]
    odd_back_near = [(next_, 0, 4, 3)]
    odd_back_takes = [
        (own, 0, 14, 0, side), (own, 1, 15, 0, side), (next_, 1, 22, 0, side), (before, 0, 21, 0, side),
        (before, 1, 19, 0, side),
    ]

    def scatter(l):
        at = rows_at(l * 72, 72, 8)
        grad = norm_grad(vm.grad_m[at, :], vm.hat_m[at, :], vm.scale_m[at, :1]).astype(BF16)
        total = dot(ld.merge_t[0], grad[:, :512])
        for k in range(1, 4):
            total = total + dot(ld.merge_t[k], grad[:, 512 * k : 512 * k + 512])
        vm.send3[l] = total.astype(BF16).reshape(4, QUARTER, 512)
        by_parity(
            lambda: start_all(third, third_near, even_back, even_back_near, l),
            lambda: start_all(third, third_near, odd_back, odd_back_near, l),
        )

    loop(2, scatter)
    loads.to_part_t.wait()
    loads.to_unit_t.wait()
    loads.to_region_t.wait()

    def fourth(l):
        return [
            remote(
                vm.send4.at[l, pl.ds(at, size)],
                vm.region4.at[l, pl.ds(128 + at, size)],
                23 + n,
                l,
                device(-to[0], -to[1]),
            )
            for n, (at, size, to) in enumerate(pieces)
        ]

    def fine_backward(l):
        base = l * 320
        level = rows_at(base, 320)
        by_parity(
            lambda: take_all(third, third_near, even_back_takes, even_back_near, l),
            lambda: take_all(third, third_near, odd_back_takes, odd_back_near, l),
        )
        vm.dmixed[level, :] = dot(ld.to_part_t[...], vm.part[l].reshape(2 * PART, 512)).astype(BF16)
        grad = dot_nt(vm.dmixed[level, :], ld.fine_out[...]) * vm.recip_f[level, :]
        vm.dheads_f[level, :] = grad.astype(BF16)
        vm.dprod_f[level, :] = (grad * vm.heads_f[level, :].astype(F32)).astype(BF16)

        def fine_attend_grad(m):
            at, wide = rows_at(base + m * UNIT, UNIT), rows_at(base + m * UNIT, 128)
            pairs = [slice(128 * p, 128 * p + 128) for p in range(4)]
            minus = jnp.full((128, 128), -1.0, BF16)
            grads = [two_heads(vm.dheads_f[at, pair], vm.heads2) for pair in pairs]
            prods = [two_heads(vm.dprod_f[at, pair], vm.heads2) for pair in pairs]
            queries = [two_heads(vm.proj[at, pair], vm.heads2) for pair in pairs]
            inner = [
                dot_nt(
                    jnp.concatenate([g, d], axis=1),
                    jnp.concatenate([vm.proj[wide, 1024 + pair.start : 1024 + pair.stop], minus], axis=1),
                )
                for pair, g, d in zip(pairs, grads, prods)
            ]
            raised = [vm.raised_f[l * 4 + m, p] for p in range(4)]
            dscores = [(e.astype(F32) * x).astype(BF16) for e, x in zip(raised, inner)]
            dvalues = [dot_tn(e, g) for e, g in zip(raised, grads)]
            dkeys = [dot_tn(ds, q) for ds, q in zip(dscores, queries)]
            dqueries = [
                dot(ds, vm.proj[wide, 512 + pair.start : 512 + pair.stop]) for pair, ds in zip(pairs, dscores)
            ]
            for p, pair in enumerate(pairs):
                vm.dproj_f[at, pair] = (one_row(dqueries[p]) * 0.125).astype(BF16)
                vm.dproj_f[at, 512 + pair.start : 512 + pair.stop] = dkeys[p][:UNIT].astype(BF16)
                vm.dproj_f[at, 1024 + pair.start : 1024 + pair.stop] = dvalues[p][:UNIT].astype(BF16)

        loop(4, fine_attend_grad)
        grad = dot_nt(vm.dproj_f[level, :], ld.fine_qkv[...])
        grad = norm_grad(grad, vm.hat_f[level, :], vm.scale_f[level, :1])
        dunit = (vm.dmixed[level, :].astype(F32) + grad).astype(BF16)
        ordered = dot(ld.to_unit_t[...], dunit).astype(BF16)
        vm.region4[l, :128, :] = ordered[:128]
        vm.send4[l] = ordered[128:]
        for copy in fourth(l):
            copy.start()

    loop(2, fine_backward)
    result_near.wait()
    result_far.wait()

    def grid_back(l):
        for copy in fourth(l):
            copy.wait()
        rows = dot(ld.to_region_t[...], vm.region4[l]).astype(BF16)
        grad_ref[l] = rows.reshape(24, 16, 512)[:, :12]
        by_parity(
            lambda: (sent_all(second, even_sends, l), sent_all(third, even_back, l)),
            lambda: (sent_all(second, odd_sends, l), sent_all(third, odd_back, l)),
        )

    loop(2, grid_back)


def per_device(n_lat, n_lon, *args):
    operands = list(args) + [jnp.asarray(m) for m in row_orders()]
    shapes = dict(zip(ARGS, [(x.shape, x.dtype) for x in operands]))
    loaded = [
        pltpu.VMEM(shapes[name][0][1:] if paired else shapes[name][0], shapes[name][1])
        for name, paired in LOADED.items()
    ]
    return pl.pallas_call(
        functools.partial(kernel, n_lat, n_lon),
        out_shape=(
            jax.ShapeDtypeStruct((2, 12, 6, 1024), BF16),
            jax.ShapeDtypeStruct((2, 24, 12, 512), BF16),
        ),
        in_specs=[
            pl.BlockSpec(memory_space=pltpu.VMEM if placed == 1 else pl.ANY) for placed in ARGS.values()
        ],
        out_specs=(pl.BlockSpec(memory_space=pltpu.VMEM), pl.BlockSpec(memory_space=pltpu.VMEM)),
        scratch_shapes=[pltpu.VMEM(*spec) for spec in SCRATCH.values()]
        + loaded
        + [
            pltpu.SemaphoreType.DMA((len(LOADED),)),
            pltpu.SemaphoreType.DMA((26, 2)),
            pltpu.SemaphoreType.DMA((26, 2)),
            pltpu.SemaphoreType.DMA((6, 2)),
        ],
        compiler_params=pltpu.CompilerParams(
            collective_id=0, has_side_effects=True, vmem_limit_bytes=60 * 2**20
        ),
    )(*operands)


def solution(mesh):
    grid = P(None, "lat", "lon", None)
    placed = (grid, P(None, "lat", "lon"), P(), P(), P(), P(), P(), P(), P(), grid)
    return jax.shard_map(
        functools.partial(per_device, mesh.shape["lat"], mesh.shape["lon"]),
        mesh=mesh,
        in_specs=placed,
        out_specs=(grid, grid),
        check_vma=False,
    )
```

profile of v0, /device:TPU:0, one launch (start us, length us, event | category | flops | bytes accessed | tf_op | source)
XLA Modules:
  0.0 79.8 jit_solution(12547008502635675088)
XLA Ops:
  0.6 1.4 %copy.25.refs_1_ = s32[2,24,12]{2,1,0:T(8,128)} copy(s32[2,24,12]{1,0,2:T(2,128)} %param.23) | data formatting | bytes 4608 | tf_op args[1]
  2.0 1.8 %copy.26.refs_9_ = bf16[2,12,6,1024]{3,2,1,0:T(8,128)(2,1)} copy(bf16[2,12,6,1024]{3,0,2,1:T(2,128)(2,1)} %param.31) | data formatting | bytes 589824 | tf_op args[9]
  3.8 2.1 %copy.24.refs_0_ = bf16[2,24,12,512]{3,2,1,0:T(8,128)(2,1)} copy(bf16[2,24,12,512]{3,1,2,0:T(8,128)(2,1)} %param.22) | data formatting | bytes 1179648 | tf_op args[0]
  6.0 69.6 %shard_map.221 = (bf16[2,12,6,1024]{3,2,1,0:T(8,128)(2,1)}, bf16[2,24,12,512]{3,2,1,0:T(8,128)(2,1)}) custom-call(bf16[2,24,12,512]{3,2,1,0:T(8,128)(2,1)} %copy.24.refs_0_, s32[2,24,12]{2,1,0:T(8,128)} %copy.25.refs_1_, f32[8,144,144]{2,1,0:T(8,128)} %refs_2_.1, bf16[512,1536]{1,0:T(8,128)(2,1)} %refs_3_.1, bf16[512,512]{1,0:T(8,128)(2,1)} %refs_4_.1, ...), custom_call_target="tpu_custom_call" | custom-call | tf_op jit(solution)/shard_map/pallas_call | solution.py:685
  75.5 2.0 %copy.27 = bf16[2,12,6,1024]{3,0,2,1:T(2,128)(2,1)} copy(bf16[2,12,6,1024]{3,2,1,0:T(8,128)(2,1)} %get-tuple-element.2) | data formatting | bytes 589824 | tf_op jit(solution)/shard_map/pallas_call | solution.py:685
  77.6 2.3 %copy.28 = bf16[2,24,12,512]{3,1,2,0:T(8,128)(2,1)} copy(bf16[2,24,12,512]{3,2,1,0:T(8,128)(2,1)} %get-tuple-element.3) | data formatting | bytes 1179648 | tf_op jit(solution)/shard_map/pallas_call | solution.py:685
where the time goes:
time: 80.2 us; the launch traced here: 79.8 us
  Pallas kernels  69.6 us (87%)
  local copies, waits for them, and re-layouts  9.62 us (12%)
    pallas_call x1, Pallas kernels, per_device(): pl.pallas_call(functools.partial(kernel, n_lat, n_lon), out_shape=(jax.Sh...  69.6 us
    unnamed x3, local copies, waits for them, and re-layouts  5.33 us
    pallas_call x2, local copies, waits for them, and re-layouts, per_device(): pl.pallas_call(functools.partial(kernel, n_lat, n_lon), out_shape=(jax.Sh...  4.29 us

commit v1 on v0

--- a/solution.py
+++ b/solution.py
@@ -46,7 +46,7 @@
 
 @functools.cache
 def row_orders():
-    to_region = one_hot([(region_of(r, c), r * 16 + c) for r in range(24) for c in range(12)], 320, 384)
+    to_region = one_hot([(region_of(r, c), c * 24 + r) for r in range(24) for c in range(12)], 320, 288)
     unit_pairs, part_pairs = [], []
     for s in range(24):
         for o in range(12):
@@ -69,15 +69,15 @@
                     merge[u, k, r * 12 + c, quarter * QUARTER + at] = 1.0
     coarse = one_hot(
         [
-            (l * 72 + r * 12 + c, (((c // 6) * 2 + l) * 6 + r) * 16 + c % 6)
+            (l * 72 + r * 12 + c, (((c // 6) * 6 + r) * 6 + c % 6) * 2 + l)
             for l in range(2)
             for r in range(6)
             for c in range(12)
         ],
         144,
-        384,
+        144,
     )
-    id_row = one_hot([(t, t // 12 + 2) for t in range(72)], UNIT, 8)
+    id_row = one_hot([(t, t // 12 + 18) for t in range(72)], UNIT, 24)
     id_col = one_hot([(t, t % 12) for t in range(72)], UNIT, 12)
     both = lambda m: [m, np.swapaxes(m, -1, -2)]
     orders = both(to_region) + both(to_unit) + both(to_part) + both(merge) + both(coarse)
@@ -132,12 +132,11 @@
     merge=0, merge_t=0, coarse=0, coarse_t=0, id_row=1, id_col=1,
 )
 LOADED = dict(
-    tokens=0, to_region=0, to_unit=0, fine_bias=0, fine_qkv=0, fine_out=0, to_part=0, coarse=0, coarse_bias=0,
-    merge=1, merge_weight=0, coarse_qkv=0, coarse_out=0, coarse_t=0, merge_t=1, to_part_t=0, to_unit_t=0,
+    tokens=0, to_region=0, fine_bias=0, coarse=0, coarse_bias=0, coarse_out=0, to_unit=0, fine_qkv=0, fine_out=0,
+    to_part=0, merge=1, merge_weight=0, coarse_qkv=0, coarse_t=0, merge_t=1, to_part_t=0, to_unit_t=0,
     to_region_t=0,
 )
 SCRATCH = dict(
-    x16=((2, 24, 16, 512), BF16),
     heads2=((160, 128), BF16),
     heads2_c=((288, 128), BF16),
     send1=((2, 192, 512), BF16),
@@ -166,9 +165,8 @@
     recip_c=((144, 1024), F32),
     heads_c=((144, 1024), BF16),
     result=((144, 1024), BF16),
-    result16=((2, 2, 6, 6, 1024), BF16),
-    cot_raw=((2, 2, 6, 6, 1024), BF16),
-    cot16=((2, 2, 6, 16, 1024), BF16),
+    result2=((2, 6, 6, 2, 1024), BF16),
+    cot2=((2, 6, 6, 2, 1024), BF16),
     cot=((144, 1024), BF16),
     dheads_c=((144, 1024), BF16),
     dprod_c=((144, 1024), BF16),
@@ -224,12 +222,10 @@
         copy.start()
         setattr(loads, name, copy)
     own_cot = pltpu.make_async_copy(
-        hbm.cotangent.at[:, pl.ds(6 * odd, 6)], vm.cot_raw.at[odd], near_sem.at[0, 0]
+        hbm.cotangent.at[pl.ds(6 * odd, 6)], vm.cot2.at[odd], near_sem.at[0, 0]
     )
     own_cot.start()
 
-    vm.x16[:, :, 12:, :] = jnp.zeros((2, 24, 4, 512), BF16)
-    vm.cot16[:, :, :, 6:, :] = jnp.zeros((2, 2, 6, 10, 1024), BF16)
     for end in (320, 640):
         vm.proj[end : end + 64, :] = jnp.zeros((64, 1536), BF16)
     vm.proj_c[144:, :] = jnp.zeros((112, 3072), BF16)
@@ -243,7 +239,6 @@
 
     loads.tokens.wait()
     loads.to_region.wait()
-    vm.x16[:, :, :12, :] = ld.tokens[...]
     pl.semaphore_wait(barrier, len(NEIGHBOURS))
     pieces = [(0, 128, (0, -1)), (128, 32, (-1, 0)), (160, 32, (-1, -1))]
 
@@ -256,7 +251,7 @@
         ]
 
     def regions(l):
-        ordered = dot(ld.to_region[...], vm.x16[l].reshape(384, 512)).astype(BF16)
+        ordered = dot(ld.to_region[...], ld.tokens[l]).astype(BF16)
         vm.region[l, :128, :] = ordered[:128]
         vm.send1[l] = ordered[128:]
         for copy in first(l):
@@ -264,7 +259,7 @@
 
     loop(2, regions)
     partner_cot = remote(
-        hbm.cotangent.at[:, pl.ds(6 - 6 * odd, 6)], vm.cot_raw.at[odd], 3, 0, device(0, 1 - 2 * odd)
+        hbm.cotangent.at[pl.ds(6 - 6 * odd, 6)], vm.cot2.at[odd], 3, 0, device(0, 1 - 2 * odd)
     )
     partner_cot.start()
 
@@ -273,8 +268,8 @@
     subs = lax.broadcasted_iota(jnp.int32, (UNIT, 128), 0)
     past = jnp.where(lanes >= 72, MASKED, 0.0).astype(F32)
     for level in range(2):
-        spread = dot(hbm.id_row[...], hbm.mask_ids[level, 16:24, :].astype(F32))
-        id_of = jnp.sum(spread * hbm.id_col[...], axis=-1, keepdims=True)
+        spread = dot(hbm.id_col[...], hbm.mask_ids[:, level, :].astype(F32))
+        id_of = jnp.sum(spread * hbm.id_row[...], axis=-1, keepdims=True)
         id_at = dot(jnp.ones((8, UNIT), F32), jnp.where(lanes == subs, id_of, 0.0))[:1]
         apart = jnp.where(id_of == id_at, past, MASKED)
         for head in range(8):
@@ -292,6 +287,17 @@
         vm.bias_c[h] = jnp.concatenate([ld.coarse_bias[h], jnp.full((144, 112), MASKED, F32)], axis=1)
 
     loop(16, coarse_pad)
+    own_cot.wait()
+    partner_cot.wait()
+    loads.coarse.wait()
+    vm.cot[...] = dot(ld.coarse[...], vm.cot2[...].reshape(144, 1024)).astype(BF16)
+    loads.coarse_out.wait()
+
+    def coarse_cot(t):
+        cols = rows_at(t * 512, 512, 512)
+        vm.grad_c[:, cols] = dot_nt(vm.cot[...], ld.coarse_out[cols, :])
+
+    loop(2, coarse_cot)
     loads.to_unit.wait()
     loads.fine_qkv.wait()
     loads.fine_out.wait()
@@ -408,22 +414,10 @@
 
     loop(2, fine_forward)
 
-    own_cot.wait()
-    partner_cot.wait()
-    loads.coarse.wait()
-    vm.cot16[:, :, :, :6, :] = vm.cot_raw[...]
-    vm.cot[...] = dot(ld.coarse[...], vm.cot16[...].reshape(384, 1024)).astype(BF16)
-    loads.coarse_out.wait()
     loads.merge.wait()
     loads.merge_weight.wait()
     loads.coarse_qkv.wait()
     loads.coarse_t.wait()
-
-    def coarse_cot(t):
-        cols = rows_at(t * 512, 512, 512)
-        vm.grad_c[:, cols] = dot_nt(vm.cot[...], ld.coarse_out[cols, :])
-
-    loop(2, coarse_cot)
 
     def gather(l):
         by_parity(
@@ -502,14 +496,10 @@
 
     loop(2, coarse_mix)
 
-    def spread_result(h):
-        rows = dot(ld.coarse_t[rows_at(h * 192, 192), :], vm.result[...]).astype(BF16)
-        vm.result16[h] = rows.reshape(2, 6, 16, 1024)[:, :, :6]
-
-    loop(2, spread_result)
-    into = result_ref.at[:, pl.ds(6 * odd, 6)]
-    result_near = pltpu.make_async_copy(vm.result16.at[odd], into, near_sem.at[3, 0])
-    result_far = remote(vm.result16.at[1 - odd], into, 13, 0, device(0, 1 - 2 * odd))
+    vm.result2[...] = dot(ld.coarse_t[...], vm.result[...]).astype(BF16).reshape(2, 6, 6, 2, 1024)
+    into = result_ref.at[pl.ds(6 * odd, 6)]
+    result_near = pltpu.make_async_copy(vm.result2.at[odd], into, near_sem.at[3, 0])
+    result_far = remote(vm.result2.at[1 - odd], into, 13, 0, device(0, 1 - 2 * odd))
     result_near.start()
     result_far.start()
 
@@ -665,8 +655,7 @@
     def grid_back(l):
         for copy in fourth(l):
             copy.wait()
-        rows = dot(ld.to_region_t[...], vm.region4[l]).astype(BF16)
-        grad_ref[l] = rows.reshape(24, 16, 512)[:, :12]
+        grad_ref[l] = dot(ld.to_region_t[...], vm.region4[l]).astype(BF16)
         by_parity(
             lambda: (sent_all(second, even_sends, l), sent_all(third, even_back, l)),
             lambda: (sent_all(second, odd_sends, l), sent_all(third, odd_back, l)),
@@ -676,17 +665,20 @@
 
 
 def per_device(n_lat, n_lon, *args):
-    operands = list(args) + [jnp.asarray(m) for m in row_orders()]
+    tokens, mask_ids, *middle, cotangent = args
+    tokens = tokens.transpose(0, 2, 1, 3).reshape(2, 288, 512)
+    operands = [tokens, mask_ids.transpose(2, 0, 1), *middle, cotangent.transpose(1, 2, 0, 3)]
+    operands += [jnp.asarray(m) for m in row_orders()]
     shapes = dict(zip(ARGS, [(x.shape, x.dtype) for x in operands]))
     loaded = [
         pltpu.VMEM(shapes[name][0][1:] if paired else shapes[name][0], shapes[name][1])
         for name, paired in LOADED.items()
     ]
-    return pl.pallas_call(
+    result, grad = pl.pallas_call(
         functools.partial(kernel, n_lat, n_lon),
         out_shape=(
-            jax.ShapeDtypeStruct((2, 12, 6, 1024), BF16),
-            jax.ShapeDtypeStruct((2, 24, 12, 512), BF16),
+            jax.ShapeDtypeStruct((12, 6, 2, 1024), BF16),
+            jax.ShapeDtypeStruct((2, 288, 512), BF16),
         ),
         in_specs=[
             pl.BlockSpec(memory_space=pltpu.VMEM if placed == 1 else pl.ANY) for placed in ARGS.values()
@@ -704,6 +696,7 @@
             collective_id=0, has_side_effects=True, vmem_limit_bytes=60 * 2**20
         ),
     )(*operands)
+    return result.transpose(2, 0, 1, 3), grad.reshape(2, 12, 24, 512).transpose(0, 2, 1, 3)
 
 
 def solution(mesh):

time: 80.2 us -> 74.3 us (0.926)
  local copies, waits for them, and re-layouts: 9.62 us -> 3.8 us
    pallas_call x2 -> x0, local copies, waits for them, and re-layouts: 4.29 us -> none  [per_device(): pl.pallas_call(functools.partial(kernel, n_lat, n_lon), out_shape=(jax.Sh...]
    unnamed x3 -> x2, local copies, waits for them, and re-layouts: 5.33 us -> 3.8 us
where the time goes in v1:
time: 74.3 us; the launch traced here: 74 us
  Pallas kernels  69.6 us (94%)
  local copies, waits for them, and re-layouts  3.8 us (5%)
    pallas_call x1, Pallas kernels, per_device(): pl.pallas_call(functools.partial(kernel, n_lat, n_lon), out_shape=(jax.Sh...  69.6 us
    unnamed x2, local copies, waits for them, and re-layouts  3.8 us

profile of v1, /device:TPU:0, one launch (start us, length us, event | category | flops | bytes accessed | tf_op | source)
XLA Modules:
  0.0 74.0 jit_solution(858797983432836438)
XLA Ops:
  0.6 69.6 %shard_map.221 = (bf16[12,6,2,1024]{3,2,1,0:T(2,128)(2,1)}, bf16[2,288,512]{2,1,0:T(8,128)(2,1)}) custom-call(bf16[2,288,512]{2,1,0:T(8,128)(2,1)} %bitcast.9, s32[12,2,24]{2,1,0:T(2,128)} %bitcast.13, f32[8,144,144]{2,1,0:T(8,128)} %refs_2_.1, bf16[512,1536]{1,0:T(8,128)(2,1)} %refs_3_.1, bf16[512,512]{1,0:T(8,128)(2,1)} %refs_4_.1, ...), custom_call_target="tpu_custom_call" | custom-call | tf_op jit(solution)/shard_map/pallas_call | solution.py:677
  70.2 1.9 %copy.26 = bf16[2,12,6,1024]{3,0,2,1:T(2,128)(2,1)} copy(bf16[2,12,6,1024]{3,0,2,1:T(2,128)(2,1)} %bitcast.11) | data formatting | bytes 589824
  72.1 1.9 %copy.27 = bf16[2,24,12,512]{3,1,2,0:T(8,128)(2,1)} copy(bf16[2,24,12,512]{3,1,2,0:T(8,128)(2,1)} %bitcast.10) | data formatting | bytes 1179648

commit v2 on v1

v2 whole, which is shorter than its diff:
```python
import functools

import jax
import jax.numpy as jnp
import numpy as np
from jax import lax
from jax.experimental import pallas as pl
from jax.experimental.pallas import tpu as pltpu
from jax.sharding import PartitionSpec as P

F32 = jnp.float32
BF16 = jnp.bfloat16
EPSILON = 1e-05
MASKED = -1e30
MESH = pl.DeviceIdType.MESH

UNIT = 80
QUARTER = 96
NEIGHBOURS = [(a, b) for a in (-1, 0, 1) for b in (-1, 0, 1) if (a, b) != (0, 0)] + [(0, 2), (0, -2)]


def one_hot(pairs, rows, columns):
    out = np.zeros((rows, columns), np.float32)
    for r, c in pairs:
        out[r, c] = 1.0
    return out


def in_quarter(row, col):
    return row * 6 + col if row < 9 else 64 + (row - 9) * 6 + col


@functools.cache
def row_orders():
    to_region = np.zeros((2, 4 * QUARTER, 288), np.float32)
    for odd in range(2):
        for half in range(2):
            for c in range(6):
                for a in range(12):
                    col = 24 * (6 * half + c)
                    upper = a + 3
                    lower = a + 15 if a < 9 else a - 9
                    kept, sent = (lower, upper) if odd else (upper, lower)
                    to_region[odd, half * QUARTER + in_quarter(a, c), col + kept] = 1.0
                    to_region[odd, (2 + half) * QUARTER + in_quarter(a, c), col + sent] = 1.0
    to_unit = one_hot(
        [
            (UNIT * (a // 6) + 12 * (a % 6) + o, (o // 6) * QUARTER + in_quarter(a, o % 6))
            for a in range(12)
            for o in range(12)
        ],
        2 * UNIT,
        2 * QUARTER,
    )
    merge = np.zeros((4, 72, 4 * QUARTER), np.float32)
    for k, (dr, dc) in enumerate([(0, 0), (1, 0), (0, 1), (1, 1)]):
        for r in range(6):
            for c in range(12):
                quarter, col = divmod(2 * c + dc, 6)
                a = 2 * r + dr
                at = 64 + a * 6 + col if a < 3 else (a - 3) * 6 + col
                merge[k, r * 12 + c, quarter * QUARTER + at] = 1.0
    coarse = one_hot(
        [
            (l * 72 + r * 12 + c, (((c // 6) * 6 + r) * 6 + c % 6) * 2 + l)
            for l in range(2)
            for r in range(6)
            for c in range(12)
        ],
        144,
        144,
    )
    id_row = one_hot([(t, t // 12 + 18) for t in range(72)], UNIT, 24)
    id_col = one_hot([(t, t % 12) for t in range(72)], UNIT, 12)
    both = lambda m: [m, np.swapaxes(m, -1, -2)]
    orders = both(to_region) + both(to_unit) + both(merge) + both(coarse)
    return [np.ascontiguousarray(m).astype(jnp.bfloat16) for m in orders] + [id_row, id_col]


def dot(a, b):
    return lax.dot_general(a, b, (((1,), (0,)), ((), ())), preferred_element_type=F32)


def dot_nt(a, b):
    return lax.dot_general(a, b, (((1,), (1,)), ((), ())), preferred_element_type=F32)


def dot_tn(a, b):
    return lax.dot_general(a, b, (((0,), (0,)), ((), ())), preferred_element_type=F32)


def normed_rows(x):
    center = x - jnp.mean(x, axis=-1, keepdims=True)
    scale = lax.rsqrt(jnp.mean(center * center, axis=-1, keepdims=True) + EPSILON)
    return center * scale, scale


def norm_grad(grad, hat, scale):
    inner = jnp.mean(grad * hat, axis=-1, keepdims=True)
    return scale * (grad - jnp.mean(grad, axis=-1, keepdims=True) - hat * inner)


def one_row(x):
    span = x.shape[0] // 2
    low = lax.broadcasted_iota(jnp.int32, (span, 128), 1) < 64
    return jnp.where(low, x[:span], x[span:])


def rows_at(start, size, unit=16):
    return pl.ds(pl.multiple_of(start, unit), size)


def loop(count, body):
    lax.fori_loop(0, count, lambda t, c: (body(t), c)[1], 0)


class Box:
    def __init__(self, **fields):
        self.__dict__.update(fields)


ARGS = dict(
    tokens=0, mask_ids=1, fine_bias=0, fine_qkv=0, fine_out=0, merge_weight=0, coarse_bias=0, coarse_qkv=0,
    coarse_out=0, cotangent=2, to_region=0, to_region_t=0, to_unit=0, to_unit_t=0,
    merge=0, merge_t=0, coarse=0, coarse_t=0, id_row=1, id_col=1,
)
LOADED = dict(
    tokens=0, to_region=1, fine_bias=0, coarse=0, coarse_bias=0, coarse_out=0, to_unit=0, fine_qkv=0, fine_out=0,
    to_unit_t=0, merge=0, merge_weight=0, coarse_qkv=0, coarse_t=0, merge_t=0, to_region_t=1,
)
SCRATCH = dict(
    heads2=((160, 128), BF16),
    heads2_c=((288, 128), BF16),
    send1=((2, 4, QUARTER, 512), BF16),
    region=((2, 4, QUARTER, 512), BF16),
    unit_x=((640, 512), BF16),
    unit_n=((640, 512), BF16),
    hat_f=((640, 512), F32),
    scale_f=((640, 128), F32),
    proj=((704, 1536), BF16),
    mask_left=((12, 2, 24), jnp.int32),
    bias_f=((3, 2, 4, 160, 128), F32),
    raised_f=((8, 4, 160, 128), BF16),
    recip_f=((640, 512), F32),
    heads_f=((640, 512), BF16),
    send2=((2, 4, QUARTER, 512), BF16),
    quarters=((2, 4, QUARTER, 512), BF16),
    hat_m=((144, 2048), F32),
    scale_m=((144, 128), F32),
    normed_m=((144, 2048), BF16),
    merged=((144, 1024), BF16),
    hat_c=((144, 1024), F32),
    scale_c=((144, 128), F32),
    normed_c=((144, 1024), BF16),
    proj_c=((256, 3072), BF16),
    bias_c=((16, 144, 256), F32),
    raised_c=((8, 288, 256), BF16),
    recip_c=((144, 1024), F32),
    heads_c=((144, 1024), BF16),
    result=((144, 1024), BF16),
    result2=((2, 6, 6, 2, 1024), BF16),
    cot2=((2, 6, 6, 2, 1024), BF16),
    cot=((144, 1024), BF16),
    dheads_c=((144, 1024), BF16),
    dprod_c=((144, 1024), BF16),
    dproj_c=((144, 3072), BF16),
    grad_c=((144, 1024), F32),
    dmerged=((144, 1024), BF16),
    grad_m=((144, 2048), F32),
    send3=((2, 4, QUARTER, 512), BF16),
    part=((2, 4, QUARTER, 512), BF16),
    dmixed=((640, 512), BF16),
    dheads_f=((640, 512), BF16),
    dprod_f=((640, 512), BF16),
    dproj_f=((640, 1536), BF16),
    send4=((2, 4, QUARTER, 512), BF16),
    region4=((2, 4, QUARTER, 512), BF16),
)
def kernel(n_lat, n_lon, *refs):
    rest = list(refs)
    hbm = Box(**{name: rest.pop(0) for name in ARGS})
    result_ref, grad_ref = rest.pop(0), rest.pop(0)
    vm = Box(**{name: rest.pop(0) for name in SCRATCH})
    ld = Box(**{name: rest.pop(0) for name in LOADED})
    load_sem, send_sem, recv_sem, near_sem = rest

    i, j = lax.axis_index("lat"), lax.axis_index("lon")
    odd = lax.rem(j, 2)
    even = odd == 0

    def device(di, dj):
        return (lax.rem(i + di + n_lat, n_lat), lax.rem(j + dj + n_lon, n_lon))

    def remote(src, dst, sem, l, target):
        return pltpu.make_async_remote_copy(
            src_ref=src,
            dst_ref=dst,
            send_sem=send_sem.at[sem, l],
            recv_sem=recv_sem.at[sem, l],
            device_id=target,
            device_id_type=MESH,
        )

    vm.mask_left[...] = jnp.zeros((12, 2, 24), jnp.int32)
    barrier = pltpu.get_barrier_semaphore()
    for di, dj in NEIGHBOURS:
        pl.semaphore_signal(barrier, inc=1, device_id=device(di, dj), device_id_type=MESH)

    loads = Box()
    for at, (name, paired) in enumerate(LOADED.items()):
        src = getattr(hbm, name)
        if paired:
            src = src.at[odd]
        copy = pltpu.make_async_copy(src, getattr(ld, name), load_sem.at[at])
        copy.start()
        setattr(loads, name, copy)
    own_cot = pltpu.make_async_copy(
        hbm.cotangent.at[pl.ds(6 * odd, 6)], vm.cot2.at[odd], near_sem.at[16, 0]
    )
    own_cot.start()

    for end in (320, 640):
        vm.proj[end : end + 64, :] = jnp.zeros((64, 1536), BF16)
    vm.proj_c[144:, :] = jnp.zeros((112, 3072), BF16)
    for ref in (vm.heads2, vm.heads2_c):
        low = lax.broadcasted_iota(jnp.int32, ref.shape, 1) < 64
        first = lax.broadcasted_iota(jnp.int32, ref.shape, 0) < ref.shape[0] // 2
        ref[...] = jnp.where(low == first, 1.0, 0.0).astype(BF16)

    def two_heads(x, mask):
        return jnp.concatenate([x, x], axis=0) * mask[...]

    loads.tokens.wait()
    loads.to_region.wait()
    pl.semaphore_wait(barrier, len(NEIGHBOURS))

    whole, top, low = (0, 96), (0, 64), (64, 32)
    left, right, far_left, far_right = (0, -1), (0, 1), (0, -2), (0, 2)
    plans = [
        (
            vm.send1,
            vm.region,
            [
                (2, 3, low, (-1, -1)), (3, 0, low, (-1, 1)), (2, 3, top, left), (3, 0, top, right),
                (0, 1, whole, None), (1, 2, whole, None),
            ],
            [
                (0, 1, low, (-1, 0)), (1, 2, low, (-1, 0)), (2, 3, whole, left), (3, 0, whole, right),
                (0, 1, top, None), (1, 2, top, None),
            ],
        ),
        (
            vm.send2,
            vm.quarters,
            [
                (0, 3, top, far_left), (0, 3, low, left), (1, 0, low, right), (2, 1, low, right),
                (3, 2, low, right), (1, 0, top, None), (2, 1, top, None), (3, 2, top, None),
            ],
            [
                (3, 0, top, far_right), (3, 0, low, (1, 1)), (0, 1, low, (1, -1)), (1, 2, low, (1, -1)),
                (2, 3, low, (1, -1)), (0, 1, top, None), (1, 2, top, None), (2, 3, top, None),
            ],
        ),
    ]
    for (_, _, of_even, of_odd), src, dst in ((plans[1], vm.send3, vm.part), (plans[0], vm.send4, vm.region4)):
        back_even, back_odd = [], []
        for mine, ours in ((of_even, 0), (of_odd, 1)):
            for at, into, rows, to in mine:
                if to is None:
                    target = ours
                    way = None
                else:
                    target = (ours + to[1]) % 2
                    way = (-to[0], -to[1])
                (back_odd if target else back_even).append((into, at, rows, way))
        plans.append((src, dst, back_even, back_odd))

    def transfer(phase, l, plan):
        at, into, (start, size), to = plan
        src, dst = plans[phase][:2]
        src, dst = src.at[l, at, pl.ds(start, size)], dst.at[l, into, pl.ds(start, size)]
        sem = phase * 8 + into * 2 + (start > 0)
        if to is None:
            return pltpu.make_async_copy(src, dst, near_sem.at[phase * 4 + into, l])
        return remote(src, dst, sem, l, device(*to))

    def by_parity(of_even, of_odd):
        @pl.when(even)
        def _():
            of_even()

        @pl.when(odd == 1)
        def _():
            of_odd()

    def send(phase, l, keep=None):
        def start(mine):
            for plan in mine:
                if keep is None or plan[0] in keep:
                    transfer(phase, l, plan).start()

        by_parity(lambda: start(plans[phase][2]), lambda: start(plans[phase][3]))

    def arrivals(phase, parity):
        got = []
        for ours in range(2):
            for plan in plans[phase][2 + ours]:
                to = plan[3]
                if (ours if to is None else (ours + to[1]) % 2) == parity:
                    got.append(plan)
        return got

    def take(phase, l, keep=None):
        def wait(parity):
            for plan in arrivals(phase, parity):
                if keep is None or plan[1] in keep:
                    copy = transfer(phase, l, plan)
                    copy.wait() if plan[3] is None else copy.wait_recv()

        by_parity(lambda: wait(0), lambda: wait(1))

    def sent(phase, l):
        def wait(mine):
            for plan in mine:
                if plan[3] is not None:
                    transfer(phase, l, plan).wait_send()

        by_parity(lambda: wait(plans[phase][2]), lambda: wait(plans[phase][3]))

    def at_strip(strip, of_strip):
        @pl.when(strip == 0)
        def _():
            of_strip((0, 1))

        @pl.when(strip == 1)
        def _():
            of_strip((2, 3))

    def regions(l):
        vm.send1[l] = dot(ld.to_region[...], ld.tokens[l]).astype(BF16).reshape(4, QUARTER, 512)
        send(0, l)

    loop(2, regions)
    partner_cot = remote(
        hbm.cotangent.at[pl.ds(6 - 6 * odd, 6)], vm.cot2.at[odd], 32, 0, device(0, 1 - 2 * odd)
    )
    partner_cot.start()
    left_mask = remote(hbm.mask_ids, vm.mask_left, 34, 0, device(0, 1))
    by_parity(left_mask.start, lambda: None)

    loads.fine_bias.wait()
    by_parity(lambda: None, left_mask.wait_recv)
    lanes = lax.broadcasted_iota(jnp.int32, (UNIT, 128), 1)
    subs = lax.broadcasted_iota(jnp.int32, (UNIT, 128), 0)
    past = jnp.where(lanes >= 72, MASKED, 0.0).astype(F32)
    for level in range(2):
        masks = [past]
        for ids in (vm.mask_left, hbm.mask_ids):
            spread = dot(hbm.id_col[...], ids[:, level, :].astype(F32))
            id_of = jnp.sum(spread * hbm.id_row[...], axis=-1, keepdims=True)
            id_at = dot(jnp.ones((8, UNIT), F32), jnp.where(lanes == subs, id_of, 0.0))[:1]
            masks.append(jnp.where(id_of == id_at, past, MASKED))
        for head in range(8):
            span = slice(72 * level, 72 * level + 72)
            block = ld.fine_bias[head, span, span]
            block = jnp.concatenate([block, jnp.zeros((72, 56), F32)], axis=1)
            block = jnp.concatenate([block, jnp.zeros((8, 128), F32)], axis=0)
            at = slice(UNIT * (head % 2), UNIT * (head % 2) + UNIT)
            for kind, mask in enumerate(masks):
                vm.bias_f[kind, level, head // 2, at, :] = block + mask

    loads.coarse_bias.wait()

    def coarse_pad(h):
        vm.bias_c[h] = jnp.concatenate([ld.coarse_bias[h], jnp.full((144, 112), MASKED, F32)], axis=1)

    loop(16, coarse_pad)
    own_cot.wait()
    partner_cot.wait()
    loads.coarse.wait()
    vm.cot[...] = dot(ld.coarse[...], vm.cot2[...].reshape(144, 1024)).astype(BF16)
    loads.coarse_out.wait()

    def coarse_cot(t):
        cols = rows_at(t * 512, 512, 512)
        vm.grad_c[:, cols] = dot_nt(vm.cot[...], ld.coarse_out[cols, :])

    loop(2, coarse_cot)
    loads.to_unit.wait()
    loads.fine_qkv.wait()
    loads.fine_out.wait()
    loads.to_unit_t.wait()

    def fine_forward(turn):
        strip = lax.rem(1 - odd + turn, 2)
        base = strip * 320
        level_at = lambda l: rows_at(base + l * 160, 160)
        both_levels = rows_at(base, 320)
        at_strip(strip, lambda keep: [take(0, l, keep) for l in range(2)])

        def fine_norm(l):
            source = vm.region[l, pl.ds(2 * strip, 2)].reshape(2 * QUARTER, 512)
            x = dot(ld.to_unit[...], source)
            hat, scale = normed_rows(x)
            vm.unit_x[level_at(l), :] = x.astype(BF16)
            vm.hat_f[level_at(l), :] = hat
            vm.scale_f[level_at(l), :] = jnp.broadcast_to(scale, (160, 128))
            vm.unit_n[level_at(l), :] = hat.astype(BF16)

        loop(2, fine_norm)

        def fine_project(t):
            cols = rows_at(t * 512, 512, 512)
            scale = jnp.where(t < 1, 0.125, 1.0).astype(F32)
            vm.proj[both_levels, cols] = (
                dot(vm.unit_n[both_levels, :], ld.fine_qkv[:, cols]) * scale
            ).astype(BF16)

        loop(3, fine_project)

        def fine_level(l):
            def fine_attend(m):
                last = odd * m * (1 + strip)
                start = base + l * 160 + m * UNIT
                at, wide = rows_at(start, UNIT), rows_at(start, 128)
                pairs = [slice(128 * p, 128 * p + 128) for p in range(4)]
                ones = jnp.ones((128, 128), BF16)
                scores = [
                    dot_nt(
                        two_heads(vm.proj[at, pair], vm.heads2), vm.proj[wide, 512 + pair.start : 512 + pair.stop]
                    )
                    + vm.bias_f[last, 1 - l, p]
                    for p, pair in enumerate(pairs)
                ]
                tops = [jnp.max(s, axis=-1, keepdims=True) for s in scores]
                raised = [jnp.exp(s - t).astype(BF16) for s, t in zip(scores, tops)]
                sums = [
                    dot(e, jnp.concatenate([vm.proj[wide, 1024 + pair.start : 1024 + pair.stop], ones], axis=1))
                    for e, pair in zip(raised, pairs)
                ]
                for p, pair in enumerate(pairs):
                    recip = 1.0 / one_row(sums[p][:, 128:])
                    vm.raised_f[strip * 4 + l * 2 + m, p] = raised[p]
                    vm.recip_f[at, pair] = recip
                    vm.heads_f[at, pair] = (one_row(sums[p][:, :128]) * recip).astype(BF16)

            loop(2, fine_attend)
            mixed = vm.unit_x[level_at(l), :].astype(F32) + dot(vm.heads_f[level_at(l), :], ld.fine_out[...])
            ordered = dot(ld.to_unit_t[...], mixed.astype(BF16)).astype(BF16)
            vm.send2[l, pl.ds(2 * strip, 2)] = ordered.reshape(2, QUARTER, 512)
            at_strip(strip, lambda keep: send(1, l, keep))

        loop(2, fine_level)

    loop(2, fine_forward)
    loads.merge.wait()
    loads.merge_weight.wait()
    loads.coarse_qkv.wait()
    loads.coarse_t.wait()

    def gather(l):
        take(1, l)
        source = vm.quarters[l].reshape(4 * QUARTER, 512)
        for k in range(4):
            vm.hat_m[rows_at(l * 72, 72, 8), 512 * k : 512 * k + 512] = dot(ld.merge[k], source)

    loop(2, gather)

    def merge_norm(t):
        at = rows_at(t * 48, 48)
        hat, scale = normed_rows(vm.hat_m[at, :])
        vm.hat_m[at, :] = hat
        vm.scale_m[at, :] = jnp.broadcast_to(scale, (48, 128))
        vm.normed_m[at, :] = hat.astype(BF16)

    loop(3, merge_norm)

    def merge_project(t):
        cols = rows_at(t * 512, 512, 512)
        vm.merged[:, cols] = dot(vm.normed_m[...], ld.merge_weight[:, cols]).astype(BF16)

    loop(2, merge_project)

    def coarse_norm(t):
        at = rows_at(t * 48, 48)
        hat, scale = normed_rows(vm.merged[at, :].astype(F32))
        vm.hat_c[at, :] = hat
        vm.scale_c[at, :] = jnp.broadcast_to(scale, (48, 128))
        vm.normed_c[at, :] = hat.astype(BF16)

    loop(3, coarse_norm)

    def coarse_project(t):
        cols = rows_at(t * 512, 512, 512)
        scale = jnp.where(t < 2, 0.125, 1.0).astype(F32)
        vm.proj_c[:144, cols] = (dot(vm.normed_c[...], ld.coarse_qkv[:, cols]) * scale).astype(BF16)

    loop(6, coarse_project)

    def cols_at(p, base):
        return rows_at(p * 128 + base, 128, 128)

    def coarse_attend(t):
        pairs = [2 * t, 2 * t + 1]
        ones = jnp.ones((256, 128), BF16)
        scores = [
            dot_nt(two_heads(vm.proj_c[:144, cols_at(p, 0)], vm.heads2_c), vm.proj_c[:, cols_at(p, 1024)])
            + vm.bias_c[pl.ds(2 * p, 2)].reshape(288, 256)
            for p in pairs
        ]
        tops = [jnp.max(s, axis=-1, keepdims=True) for s in scores]
        raised = [jnp.exp(s - top).astype(BF16) for s, top in zip(scores, tops)]
        sums = [
            dot(e, jnp.concatenate([vm.proj_c[:, cols_at(p, 2048)], ones], axis=1))
            for e, p in zip(raised, pairs)
        ]
        for p, e, total in zip(pairs, raised, sums):
            recip = 1.0 / one_row(total[:, 128:])
            vm.raised_c[p] = e
            vm.recip_c[:, cols_at(p, 0)] = recip
            vm.heads_c[:, cols_at(p, 0)] = (one_row(total[:, :128]) * recip).astype(BF16)

    loop(4, coarse_attend)

    def coarse_mix(t):
        cols = rows_at(t * 512, 512, 512)
        mixed = dot(vm.heads_c[...], ld.coarse_out[:, cols])
        vm.result[:, cols] = (vm.merged[:, cols].astype(F32) + mixed).astype(BF16)
        grad = vm.grad_c[:, cols] * vm.recip_c[:, cols]
        vm.dheads_c[:, cols] = grad.astype(BF16)
        vm.dprod_c[:, cols] = (grad * vm.heads_c[:, cols].astype(F32)).astype(BF16)

    loop(2, coarse_mix)

    vm.result2[...] = dot(ld.coarse_t[...], vm.result[...]).astype(BF16).reshape(2, 6, 6, 2, 1024)
    into = result_ref.at[pl.ds(6 * odd, 6)]
    result_near = pltpu.make_async_copy(vm.result2.at[odd], into, near_sem.at[17, 0])
    result_far = remote(vm.result2.at[1 - odd], into, 33, 0, device(0, 1 - 2 * odd))
    result_near.start()
    result_far.start()

    def coarse_attend_grad(t):
        pairs = [2 * t, 2 * t + 1]
        minus = jnp.full((256, 128), -1.0, BF16)
        grads = [two_heads(vm.dheads_c[:, cols_at(p, 0)], vm.heads2_c) for p in pairs]
        prods = [two_heads(vm.dprod_c[:, cols_at(p, 0)], vm.heads2_c) for p in pairs]
        queries = [two_heads(vm.proj_c[:144, cols_at(p, 0)], vm.heads2_c) for p in pairs]
        inner = [
            dot_nt(
                jnp.concatenate([g, d], axis=1), jnp.concatenate([vm.proj_c[:, cols_at(p, 2048)], minus], axis=1)
            )
            for p, g, d in zip(pairs, grads, prods)
        ]
        dscores = [(vm.raised_c[p].astype(F32) * x).astype(BF16) for p, x in zip(pairs, inner)]
        for p, g, q, ds in zip(pairs, grads, queries, dscores):
            vm.dproj_c[:, cols_at(p, 2048)] = dot_tn(vm.raised_c[p], g)[:144].astype(BF16)
            dq = one_row(dot(ds, vm.proj_c[:, cols_at(p, 1024)]))
            vm.dproj_c[:, cols_at(p, 0)] = (dq * 0.125).astype(BF16)
            vm.dproj_c[:, cols_at(p, 1024)] = dot_tn(ds, q)[:144].astype(BF16)

    loop(4, coarse_attend_grad)

    def coarse_project_grad(t):
        cols = rows_at(t * 512, 512, 512)
        vm.grad_c[:, cols] = dot_nt(vm.dproj_c[...], ld.coarse_qkv[cols, :])

    loop(2, coarse_project_grad)

    def coarse_norm_grad(t):
        at = rows_at(t * 48, 48)
        grad = norm_grad(vm.grad_c[at, :], vm.hat_c[at, :], vm.scale_c[at, :1])
        vm.dmerged[at, :] = (vm.cot[at, :].astype(F32) + grad).astype(BF16)

    loop(3, coarse_norm_grad)

    def merge_project_grad(t):
        cols = rows_at(t * 512, 512, 512)
        vm.grad_m[:, cols] = dot_nt(vm.dmerged[...], ld.merge_weight[cols, :])

    loop(4, merge_project_grad)
    loads.merge_t.wait()

    def scatter(l):
        at = rows_at(l * 72, 72, 8)
        grad = norm_grad(vm.grad_m[at, :], vm.hat_m[at, :], vm.scale_m[at, :1]).astype(BF16)
        total = dot(ld.merge_t[0], grad[:, :512])
        for k in range(1, 4):
            total = total + dot(ld.merge_t[k], grad[:, 512 * k : 512 * k + 512])
        vm.send3[l] = total.astype(BF16).reshape(4, QUARTER, 512)
        send(2, l)

    loop(2, scatter)
    loads.to_region_t.wait()

    def fine_backward(turn):
        strip = lax.rem(1 - odd + turn, 2)
        base = strip * 320
        level_at = lambda l: rows_at(base + l * 160, 160)
        both_levels = rows_at(base, 320)
        at_strip(strip, lambda keep: [take(2, l, keep) for l in range(2)])

        def fine_units(l):
            source = vm.part[l, pl.ds(2 * strip, 2)].reshape(2 * QUARTER, 512)
            vm.dmixed[level_at(l), :] = dot(ld.to_unit[...], source).astype(BF16)

        loop(2, fine_units)
        grad = dot_nt(vm.dmixed[both_levels, :], ld.fine_out[...]) * vm.recip_f[both_levels, :]
        vm.dheads_f[both_levels, :] = grad.astype(BF16)
        vm.dprod_f[both_levels, :] = (grad * vm.heads_f[both_levels, :].astype(F32)).astype(BF16)

        def fine_level_back(l):
            def fine_attend_grad(m):
                start = base + l * 160 + m * UNIT
                at, wide = rows_at(start, UNIT), rows_at(start, 128)
                pairs = [slice(128 * p, 128 * p + 128) for p in range(4)]
                minus = jnp.full((128, 128), -1.0, BF16)
                grads = [two_heads(vm.dheads_f[at, pair], vm.heads2) for pair in pairs]
                prods = [two_heads(vm.dprod_f[at, pair], vm.heads2) for pair in pairs]
                queries = [two_heads(vm.proj[at, pair], vm.heads2) for pair in pairs]
                inner = [
                    dot_nt(
                        jnp.concatenate([g, d], axis=1),
                        jnp.concatenate([vm.proj[wide, 1024 + pair.start : 1024 + pair.stop], minus], axis=1),
                    )
                    for pair, g, d in zip(pairs, grads, prods)
                ]
                raised = [vm.raised_f[strip * 4 + l * 2 + m, p] for p in range(4)]
                dscores = [(e.astype(F32) * x).astype(BF16) for e, x in zip(raised, inner)]
                dvalues = [dot_tn(e, g) for e, g in zip(raised, grads)]
                dkeys = [dot_tn(ds, q) for ds, q in zip(dscores, queries)]
                dqueries = [
                    dot(ds, vm.proj[wide, 512 + pair.start : 512 + pair.stop]) for pair, ds in zip(pairs, dscores)
                ]
                for p, pair in enumerate(pairs):
                    vm.dproj_f[at, pair] = (one_row(dqueries[p]) * 0.125).astype(BF16)
                    vm.dproj_f[at, 512 + pair.start : 512 + pair.stop] = dkeys[p][:UNIT].astype(BF16)
                    vm.dproj_f[at, 1024 + pair.start : 1024 + pair.stop] = dvalues[p][:UNIT].astype(BF16)

            loop(2, fine_attend_grad)
            grad = dot_nt(vm.dproj_f[level_at(l), :], ld.fine_qkv[...])
            grad = norm_grad(grad, vm.hat_f[level_at(l), :], vm.scale_f[level_at(l), :1])
            dunit = (vm.dmixed[level_at(l), :].astype(F32) + grad).astype(BF16)
            ordered = dot(ld.to_unit_t[...], dunit).astype(BF16)
            vm.send4[l, pl.ds(2 * strip, 2)] = ordered.reshape(2, QUARTER, 512)
            at_strip(strip, lambda keep: send(3, l, keep))

        loop(2, fine_level_back)

    loop(2, fine_backward)
    by_parity(left_mask.wait_send, lambda: None)
    result_near.wait()
    result_far.wait()

    def grid_back(l):
        take(3, l)
        grad_ref[l] = dot(ld.to_region_t[...], vm.region4[l].reshape(4 * QUARTER, 512)).astype(BF16)
        for phase in range(4):
            sent(phase, l)

    loop(2, grid_back)


def per_device(n_lat, n_lon, *args):
    tokens, mask_ids, *middle, cotangent = args
    tokens = tokens.transpose(0, 2, 1, 3).reshape(2, 288, 512)
    operands = [tokens, mask_ids.transpose(2, 0, 1), *middle, cotangent.transpose(1, 2, 0, 3)]
    operands += [jnp.asarray(m) for m in row_orders()]
    shapes = dict(zip(ARGS, [(x.shape, x.dtype) for x in operands]))
    loaded = [
        pltpu.VMEM(shapes[name][0][1:] if paired else shapes[name][0], shapes[name][1])
        for name, paired in LOADED.items()
    ]
    result, grad = pl.pallas_call(
        functools.partial(kernel, n_lat, n_lon),
        out_shape=(
            jax.ShapeDtypeStruct((12, 6, 2, 1024), BF16),
            jax.ShapeDtypeStruct((2, 288, 512), BF16),
        ),
        in_specs=[
            pl.BlockSpec(memory_space=pltpu.VMEM if placed == 1 else pl.ANY) for placed in ARGS.values()
        ],
        out_specs=(pl.BlockSpec(memory_space=pltpu.VMEM), pl.BlockSpec(memory_space=pltpu.VMEM)),
        scratch_shapes=[pltpu.VMEM(*spec) for spec in SCRATCH.values()]
        + loaded
        + [
            pltpu.SemaphoreType.DMA((len(LOADED),)),
            pltpu.SemaphoreType.DMA((35, 2)),
            pltpu.SemaphoreType.DMA((35, 2)),
            pltpu.SemaphoreType.DMA((18, 2)),
        ],
        compiler_params=pltpu.CompilerParams(
            collective_id=0, has_side_effects=True, vmem_limit_bytes=60 * 2**20
        ),
    )(*operands)
    return result.transpose(2, 0, 1, 3), grad.reshape(2, 12, 24, 512).transpose(0, 2, 1, 3)


def solution(mesh):
    grid = P(None, "lat", "lon", None)
    placed = (grid, P(None, "lat", "lon"), P(), P(), P(), P(), P(), P(), P(), grid)
    return jax.shard_map(
        functools.partial(per_device, mesh.shape["lat"], mesh.shape["lon"]),
        mesh=mesh,
        in_specs=placed,
        out_specs=(grid, grid),
        check_vma=False,
    )
```

time: 74.3 us -> 73.9 us (level)
  Pallas kernels: 69.6 us -> 68.7 us
    pallas_call x1, Pallas kernels: 69.6 us -> 68.7 us  [per_device(): pl.pallas_call(functools.partial(kernel, n_lat, n_lon), out_shape=(jax.Sh...]
where the time goes in v2:
time: 73.9 us; the launch traced here: 73.1 us
  Pallas kernels  68.7 us (93%)
  local copies, waits for them, and re-layouts  3.8 us (5%)
    pallas_call x1, Pallas kernels, per_device(): pl.pallas_call(functools.partial(kernel, n_lat, n_lon), out_shape=(jax.Sh...  68.7 us
    unnamed x2, local copies, waits for them, and re-layouts  3.8 us

profile of v2, /device:TPU:0, one launch (start us, length us, event | category | flops | bytes accessed | tf_op | source)
XLA Modules:
  0.0 73.1 jit_solution(5671933251890425116)
XLA Ops:
  0.6 68.7 %shard_map.203 = (bf16[12,6,2,1024]{3,2,1,0:T(2,128)(2,1)}, bf16[2,288,512]{2,1,0:T(8,128)(2,1)}) custom-call(bf16[2,288,512]{2,1,0:T(8,128)(2,1)} %bitcast.9, s32[12,2,24]{2,1,0:T(2,128)} %bitcast.13, f32[8,144,144]{2,1,0:T(8,128)} %refs_2_.1, bf16[512,1536]{1,0:T(8,128)(2,1)} %refs_3_.1, bf16[512,512]{1,0:T(8,128)(2,1)} %refs_4_.1, ...), custom_call_target="tpu_custom_call" | custom-call | tf_op jit(solution)/shard_map/pallas_call | solution.py:673
  69.3 1.9 %copy.24 = bf16[2,12,6,1024]{3,0,2,1:T(2,128)(2,1)} copy(bf16[2,12,6,1024]{3,0,2,1:T(2,128)(2,1)} %bitcast.11) | data formatting | bytes 589824
  71.2 1.9 %copy.25 = bf16[2,24,12,512]{3,1,2,0:T(8,128)(2,1)} copy(bf16[2,24,12,512]{3,1,2,0:T(8,128)(2,1)} %bitcast.10) | data formatting | bytes 1179648

commit v3 on v2

--- a/solution.py
+++ b/solution.py
@@ -125,8 +125,8 @@
     merge=0, merge_t=0, coarse=0, coarse_t=0, id_row=1, id_col=1,
 )
 LOADED = dict(
-    tokens=0, to_region=1, fine_bias=0, coarse=0, coarse_bias=0, coarse_out=0, to_unit=0, fine_qkv=0, fine_out=0,
-    to_unit_t=0, merge=0, merge_weight=0, coarse_qkv=0, coarse_t=0, merge_t=0, to_region_t=1,
+    tokens=0, to_region=1, fine_bias=0, to_unit=0, fine_qkv=0, fine_out=0, to_unit_t=0, coarse=0, coarse_bias=0,
+    coarse_out=0, merge=0, merge_weight=0, coarse_qkv=0, coarse_t=0, merge_t=0, to_region_t=1,
 )
 SCRATCH = dict(
     heads2=((160, 128), BF16),
@@ -369,23 +369,6 @@
             for kind, mask in enumerate(masks):
                 vm.bias_f[kind, level, head // 2, at, :] = block + mask
 
-    loads.coarse_bias.wait()
-
-    def coarse_pad(h):
-        vm.bias_c[h] = jnp.concatenate([ld.coarse_bias[h], jnp.full((144, 112), MASKED, F32)], axis=1)
-
-    loop(16, coarse_pad)
-    own_cot.wait()
-    partner_cot.wait()
-    loads.coarse.wait()
-    vm.cot[...] = dot(ld.coarse[...], vm.cot2[...].reshape(144, 1024)).astype(BF16)
-    loads.coarse_out.wait()
-
-    def coarse_cot(t):
-        cols = rows_at(t * 512, 512, 512)
-        vm.grad_c[:, cols] = dot_nt(vm.cot[...], ld.coarse_out[cols, :])
-
-    loop(2, coarse_cot)
     loads.to_unit.wait()
     loads.fine_qkv.wait()
     loads.fine_out.wait()
@@ -453,6 +436,23 @@
         loop(2, fine_level)
 
     loop(2, fine_forward)
+    loads.coarse_bias.wait()
+
+    def coarse_pad(h):
+        vm.bias_c[h] = jnp.concatenate([ld.coarse_bias[h], jnp.full((144, 112), MASKED, F32)], axis=1)
+
+    loop(16, coarse_pad)
+    own_cot.wait()
+    partner_cot.wait()
+    loads.coarse.wait()
+    vm.cot[...] = dot(ld.coarse[...], vm.cot2[...].reshape(144, 1024)).astype(BF16)
+    loads.coarse_out.wait()
+
+    def coarse_cot(t):
+        cols = rows_at(t * 512, 512, 512)
+        vm.grad_c[:, cols] = dot_nt(vm.cot[...], ld.coarse_out[cols, :])
+
+    loop(2, coarse_cot)
     loads.merge.wait()
     loads.merge_weight.wait()
     loads.coarse_qkv.wait()
@@ -658,6 +658,27 @@
             sent(phase, l)
 
     loop(2, grid_back)
+
+
+PIECES = 2
+
+
+def hand_over(*refs):
+    ins, outs = [], []
+    for n in range(2):
+        src, dst, held = refs[n], refs[2 + n], refs[4 + n]
+        size = src.shape[0] // PIECES
+        for piece in range(PIECES):
+            at = pl.ds(piece * size, size)
+            ins.append(pltpu.make_async_copy(src.at[at], held.at[at], refs[6].at[n, piece]))
+            outs.append(pltpu.make_async_copy(held.at[at], dst.at[at], refs[7].at[n, piece]))
+    for copy in ins:
+        copy.start()
+    for before, after in zip(ins, outs):
+        before.wait()
+        after.start()
+    for copy in outs:
+        copy.wait()
 
 
 def per_device(n_lat, n_lon, *args):
@@ -692,6 +713,23 @@
             collective_id=0, has_side_effects=True, vmem_limit_bytes=60 * 2**20
         ),
     )(*operands)
+    anywhere = pl.BlockSpec(memory_space=pl.ANY)
+    result, grad = pl.pallas_call(
+        hand_over,
+        out_shape=(
+            jax.ShapeDtypeStruct((12, 6, 2, 1024), BF16),
+            jax.ShapeDtypeStruct((8, 72, 512), BF16),
+        ),
+        in_specs=[anywhere, anywhere],
+        out_specs=(anywhere, anywhere),
+        scratch_shapes=[
+            pltpu.VMEM((12, 6, 2, 1024), BF16),
+            pltpu.VMEM((8, 72, 512), BF16),
+            pltpu.SemaphoreType.DMA((2, PIECES)),
+            pltpu.SemaphoreType.DMA((2, PIECES)),
+        ],
+        compiler_params=pltpu.CompilerParams(vmem_limit_bytes=60 * 2**20),
+    )(result, grad.reshape(8, 72, 512))
     return result.transpose(2, 0, 1, 3), grad.reshape(2, 12, 24, 512).transpose(0, 2, 1, 3)
 
 

time: 73.9 us -> 71.7 us (0.970)
  local copies, waits for them, and re-layouts: 3.8 us -> 0 us
  Pallas kernels: 68.7 us -> 69.9 us
    unnamed x2 -> x0, local copies, waits for them, and re-layouts: 3.8 us -> none
    pallas_call x0 -> x1, Pallas kernels: none -> 1.99 us  [per_device(): pl.pallas_call(hand_over, out_shape=(jax.ShapeDtypeStruct((12, 6, 2, 1024...]
    pallas_call x1, Pallas kernels: 68.7 us -> 67.9 us  [per_device(): pl.pallas_call(functools.partial(kernel, n_lat, n_lon), out_shape=(jax.Sh...]
where the time goes in v3:
time: 71.7 us; the launch traced here: 70.5 us
  Pallas kernels  69.9 us (97%)
    pallas_call x1, Pallas kernels, per_device(): pl.pallas_call(functools.partial(kernel, n_lat, n_lon), out_shape=(jax.Sh...  67.9 us
    pallas_call x1, Pallas kernels, per_device(): pl.pallas_call(hand_over, out_shape=(jax.ShapeDtypeStruct((12, 6, 2, 1024...  1.99 us

profile of v3, /device:TPU:0, one launch (start us, length us, event | category | flops | bytes accessed | tf_op | source)
XLA Modules:
  0.0 70.5 jit_solution(775165996859833434)
XLA Ops:
  0.6 67.9 %shard_map.203 = (bf16[12,6,2,1024]{3,2,1,0:T(2,128)(2,1)}, bf16[2,288,512]{2,1,0:T(8,128)(2,1)}) custom-call(bf16[2,288,512]{2,1,0:T(8,128)(2,1)} %bitcast.10, s32[12,2,24]{2,1,0:T(2,128)} %bitcast.13, f32[8,144,144]{2,1,0:T(8,128)} %refs_2_.1, bf16[512,1536]{1,0:T(8,128)(2,1)} %refs_3_.1, bf16[512,512]{1,0:T(8,128)(2,1)} %refs_4_.1, ...), custom_call_target="tpu_custom_call" | custom-call | tf_op jit(solution)/shard_map/pallas_call | solution.py:694
  68.5 2.0 %shard_map.204 = (bf16[12,6,2,1024]{3,2,1,0:T(2,128)(2,1)}, bf16[8,72,512]{2,1,0:T(8,128)(2,1)}) custom-call(bf16[12,6,2,1024]{3,2,1,0:T(2,128)(2,1)} %get-tuple-element.6.refs_0_, bf16[8,72,512]{2,1,0:T(8,128)(2,1)} %bitcast.11), custom_call_target="tpu_custom_call" | custom-call | tf_op jit(solution)/shard_map/pallas_call | solution.py:717

commit v4 on v3

--- a/solution.py
+++ b/solution.py
@@ -52,14 +52,14 @@
         2 * UNIT,
         2 * QUARTER,
     )
-    merge = np.zeros((4, 72, 4 * QUARTER), np.float32)
+    merge = np.zeros((4 * 72, 4 * QUARTER), np.float32)
     for k, (dr, dc) in enumerate([(0, 0), (1, 0), (0, 1), (1, 1)]):
         for r in range(6):
             for c in range(12):
                 quarter, col = divmod(2 * c + dc, 6)
                 a = 2 * r + dr
                 at = 64 + a * 6 + col if a < 3 else (a - 3) * 6 + col
-                merge[k, r * 12 + c, quarter * QUARTER + at] = 1.0
+                merge[k * 72 + r * 12 + c, quarter * QUARTER + at] = 1.0
     coarse = one_hot(
         [
             (l * 72 + r * 12 + c, (((c // 6) * 6 + r) * 6 + c % 6) * 2 + l)
@@ -381,7 +381,7 @@
         both_levels = rows_at(base, 320)
         at_strip(strip, lambda keep: [take(0, l, keep) for l in range(2)])
 
-        def fine_norm(l):
+        for l in range(2):
             source = vm.region[l, pl.ds(2 * strip, 2)].reshape(2 * QUARTER, 512)
             x = dot(ld.to_unit[...], source)
             hat, scale = normed_rows(x)
@@ -390,50 +390,43 @@
             vm.scale_f[level_at(l), :] = jnp.broadcast_to(scale, (160, 128))
             vm.unit_n[level_at(l), :] = hat.astype(BF16)
 
-        loop(2, fine_norm)
-
-        def fine_project(t):
-            cols = rows_at(t * 512, 512, 512)
-            scale = jnp.where(t < 1, 0.125, 1.0).astype(F32)
-            vm.proj[both_levels, cols] = (
-                dot(vm.unit_n[both_levels, :], ld.fine_qkv[:, cols]) * scale
-            ).astype(BF16)
-
-        loop(3, fine_project)
-
-        def fine_level(l):
-            def fine_attend(m):
-                last = odd * m * (1 + strip)
-                start = base + l * 160 + m * UNIT
-                at, wide = rows_at(start, UNIT), rows_at(start, 128)
-                pairs = [slice(128 * p, 128 * p + 128) for p in range(4)]
-                ones = jnp.ones((128, 128), BF16)
-                scores = [
-                    dot_nt(
-                        two_heads(vm.proj[at, pair], vm.heads2), vm.proj[wide, 512 + pair.start : 512 + pair.stop]
-                    )
-                    + vm.bias_f[last, 1 - l, p]
-                    for p, pair in enumerate(pairs)
-                ]
-                tops = [jnp.max(s, axis=-1, keepdims=True) for s in scores]
-                raised = [jnp.exp(s - t).astype(BF16) for s, t in zip(scores, tops)]
-                sums = [
-                    dot(e, jnp.concatenate([vm.proj[wide, 1024 + pair.start : 1024 + pair.stop], ones], axis=1))
-                    for e, pair in zip(raised, pairs)
-                ]
-                for p, pair in enumerate(pairs):
-                    recip = 1.0 / one_row(sums[p][:, 128:])
-                    vm.raised_f[strip * 4 + l * 2 + m, p] = raised[p]
-                    vm.recip_f[at, pair] = recip
-                    vm.heads_f[at, pair] = (one_row(sums[p][:, :128]) * recip).astype(BF16)
-
-            loop(2, fine_attend)
-            mixed = vm.unit_x[level_at(l), :].astype(F32) + dot(vm.heads_f[level_at(l), :], ld.fine_out[...])
-            ordered = dot(ld.to_unit_t[...], mixed.astype(BF16)).astype(BF16)
+        projected = dot(vm.unit_n[both_levels, :], ld.fine_qkv[...])
+        vm.proj[both_levels, :512] = (projected[:, :512] * 0.125).astype(BF16)
+        vm.proj[both_levels, 512:] = projected[:, 512:].astype(BF16)
+
+        def fine_attend(n):
+            l, m = lax.div(n, 2), lax.rem(n, 2)
+            last = odd * m * (1 + strip)
+            start = base + n * UNIT
+            at, wide = rows_at(start, UNIT), rows_at(start, 128)
+            pairs = [slice(128 * p, 128 * p + 128) for p in range(4)]
+            ones = jnp.ones((128, 128), BF16)
+            scores = [
+                dot_nt(
+                    two_heads(vm.proj[at, pair], vm.heads2), vm.proj[wide, 512 + pair.start : 512 + pair.stop]
+                )
+                + vm.bias_f[last, 1 - l, p]
+                for p, pair in enumerate(pairs)
+            ]
+            tops = [jnp.max(s, axis=-1, keepdims=True) for s in scores]
+            raised = [jnp.exp(s - t).astype(BF16) for s, t in zip(scores, tops)]
+            sums = [
+                dot(e, jnp.concatenate([vm.proj[wide, 1024 + pair.start : 1024 + pair.stop], ones], axis=1))
+                for e, pair in zip(raised, pairs)
+            ]
+            for p, pair in enumerate(pairs):
+                recip = 1.0 / one_row(sums[p][:, 128:])
+                vm.raised_f[strip * 4 + n, p] = raised[p]
+                vm.recip_f[at, pair] = recip
+                vm.heads_f[at, pair] = (one_row(sums[p][:, :128]) * recip).astype(BF16)
+
+        loop(4, fine_attend)
+        mixed = vm.unit_x[both_levels, :].astype(F32) + dot(vm.heads_f[both_levels, :], ld.fine_out[...])
+        mixed = mixed.astype(BF16)
+        for l in range(2):
+            ordered = dot(ld.to_unit_t[...], mixed[160 * l : 160 * l + 160]).astype(BF16)
             vm.send2[l, pl.ds(2 * strip, 2)] = ordered.reshape(2, QUARTER, 512)
             at_strip(strip, lambda keep: send(1, l, keep))
-
-        loop(2, fine_level)
 
     loop(2, fine_forward)
     loads.coarse_bias.wait()
@@ -448,23 +441,18 @@
     vm.cot[...] = dot(ld.coarse[...], vm.cot2[...].reshape(144, 1024)).astype(BF16)
     loads.coarse_out.wait()
 
-    def coarse_cot(t):
-        cols = rows_at(t * 512, 512, 512)
-        vm.grad_c[:, cols] = dot_nt(vm.cot[...], ld.coarse_out[cols, :])
-
-    loop(2, coarse_cot)
+    vm.grad_c[...] = dot_nt(vm.cot[...], ld.coarse_out[...])
     loads.merge.wait()
     loads.merge_weight.wait()
     loads.coarse_qkv.wait()
     loads.coarse_t.wait()
 
-    def gather(l):
+    for l in range(2):
         take(1, l)
-        source = vm.quarters[l].reshape(4 * QUARTER, 512)
+    for l in range(2):
+        gathered = dot(ld.merge[...], vm.quarters[l].reshape(4 * QUARTER, 512))
         for k in range(4):
-            vm.hat_m[rows_at(l * 72, 72, 8), 512 * k : 512 * k + 512] = dot(ld.merge[k], source)
-
-    loop(2, gather)
+            vm.hat_m[72 * l : 72 * l + 72, 512 * k : 512 * k + 512] = gathered[72 * k : 72 * k + 72]
 
     def merge_norm(t):
         at = rows_at(t * 48, 48)
@@ -475,11 +463,7 @@
 
     loop(3, merge_norm)
 
-    def merge_project(t):
-        cols = rows_at(t * 512, 512, 512)
-        vm.merged[:, cols] = dot(vm.normed_m[...], ld.merge_weight[:, cols]).astype(BF16)
-
-    loop(2, merge_project)
+    vm.merged[...] = dot(vm.normed_m[...], ld.merge_weight[...]).astype(BF16)
 
     def coarse_norm(t):
         at = rows_at(t * 48, 48)
@@ -490,12 +474,9 @@
 
     loop(3, coarse_norm)
 
-    def coarse_project(t):
-        cols = rows_at(t * 512, 512, 512)
-        scale = jnp.where(t < 2, 0.125, 1.0).astype(F32)
-        vm.proj_c[:144, cols] = (dot(vm.normed_c[...], ld.coarse_qkv[:, cols]) * scale).astype(BF16)
-
-    loop(6, coarse_project)
+    projected = dot(vm.normed_c[...], ld.coarse_qkv[...])
+    vm.proj_c[:144, :1024] = (projected[:, :1024] * 0.125).astype(BF16)
+    vm.proj_c[:144, 1024:] = projected[:, 1024:].astype(BF16)
 
     def cols_at(p, base):
         return rows_at(p * 128 + base, 128, 128)
@@ -522,16 +503,11 @@
 
     loop(4, coarse_attend)
 
-    def coarse_mix(t):
-        cols = rows_at(t * 512, 512, 512)
-        mixed = dot(vm.heads_c[...], ld.coarse_out[:, cols])
-        vm.result[:, cols] = (vm.merged[:, cols].astype(F32) + mixed).astype(BF16)
-        grad = vm.grad_c[:, cols] * vm.recip_c[:, cols]
-        vm.dheads_c[:, cols] = grad.astype(BF16)
-        vm.dprod_c[:, cols] = (grad * vm.heads_c[:, cols].astype(F32)).astype(BF16)
-
-    loop(2, coarse_mix)
-
+    mixed = dot(vm.heads_c[...], ld.coarse_out[...])
+    vm.result[...] = (vm.merged[...].astype(F32) + mixed).astype(BF16)
+    grad = vm.grad_c[...] * vm.recip_c[...]
+    vm.dheads_c[...] = grad.astype(BF16)
+    vm.dprod_c[...] = (grad * vm.heads_c[...].astype(F32)).astype(BF16)
     vm.result2[...] = dot(ld.coarse_t[...], vm.result[...]).astype(BF16).reshape(2, 6, 6, 2, 1024)
     into = result_ref.at[pl.ds(6 * odd, 6)]
     result_near = pltpu.make_async_copy(vm.result2.at[odd], into, near_sem.at[17, 0])
@@ -560,11 +536,7 @@
 
     loop(4, coarse_attend_grad)
 
-    def coarse_project_grad(t):
-        cols = rows_at(t * 512, 512, 512)
-        vm.grad_c[:, cols] = dot_nt(vm.dproj_c[...], ld.coarse_qkv[cols, :])
-
-    loop(2, coarse_project_grad)
+    vm.grad_c[...] = dot_nt(vm.dproj_c[...], ld.coarse_qkv[...])
 
     def coarse_norm_grad(t):
         at = rows_at(t * 48, 48)
@@ -573,23 +545,15 @@
 
     loop(3, coarse_norm_grad)
 
-    def merge_project_grad(t):
-        cols = rows_at(t * 512, 512, 512)
-        vm.grad_m[:, cols] = dot_nt(vm.dmerged[...], ld.merge_weight[cols, :])
-
-    loop(4, merge_project_grad)
+    vm.grad_m[...] = dot_nt(vm.dmerged[...], ld.merge_weight[...])
     loads.merge_t.wait()
 
-    def scatter(l):
-        at = rows_at(l * 72, 72, 8)
-        grad = norm_grad(vm.grad_m[at, :], vm.hat_m[at, :], vm.scale_m[at, :1]).astype(BF16)
-        total = dot(ld.merge_t[0], grad[:, :512])
-        for k in range(1, 4):
-            total = total + dot(ld.merge_t[k], grad[:, 512 * k : 512 * k + 512])
-        vm.send3[l] = total.astype(BF16).reshape(4, QUARTER, 512)
+    for l in range(2):
+        at = slice(72 * l, 72 * l + 72)
+        grad = norm_grad(vm.grad_m[at, :], vm.hat_m[at, :], vm.scale_m[at, :1])
+        grad = jnp.concatenate([grad[:, 512 * k : 512 * k + 512] for k in range(4)], axis=0)
+        vm.send3[l] = dot(ld.merge_t[...], grad.astype(BF16)).astype(BF16).reshape(4, QUARTER, 512)
         send(2, l)
-
-    loop(2, scatter)
     loads.to_region_t.wait()
 
     def fine_backward(turn):
@@ -599,52 +563,49 @@
         both_levels = rows_at(base, 320)
         at_strip(strip, lambda keep: [take(2, l, keep) for l in range(2)])
 
-        def fine_units(l):
+        for l in range(2):
             source = vm.part[l, pl.ds(2 * strip, 2)].reshape(2 * QUARTER, 512)
             vm.dmixed[level_at(l), :] = dot(ld.to_unit[...], source).astype(BF16)
 
-        loop(2, fine_units)
         grad = dot_nt(vm.dmixed[both_levels, :], ld.fine_out[...]) * vm.recip_f[both_levels, :]
         vm.dheads_f[both_levels, :] = grad.astype(BF16)
         vm.dprod_f[both_levels, :] = (grad * vm.heads_f[both_levels, :].astype(F32)).astype(BF16)
 
-        def fine_level_back(l):
-            def fine_attend_grad(m):
-                start = base + l * 160 + m * UNIT
-                at, wide = rows_at(start, UNIT), rows_at(start, 128)
-                pairs = [slice(128 * p, 128 * p + 128) for p in range(4)]
-                minus = jnp.full((128, 128), -1.0, BF16)
-                grads = [two_heads(vm.dheads_f[at, pair], vm.heads2) for pair in pairs]
-                prods = [two_heads(vm.dprod_f[at, pair], vm.heads2) for pair in pairs]
-                queries = [two_heads(vm.proj[at, pair], vm.heads2) for pair in pairs]
-                inner = [
-                    dot_nt(
-                        jnp.concatenate([g, d], axis=1),
-                        jnp.concatenate([vm.proj[wide, 1024 + pair.start : 1024 + pair.stop], minus], axis=1),
-                    )
-                    for pair, g, d in zip(pairs, grads, prods)
-                ]
-                raised = [vm.raised_f[strip * 4 + l * 2 + m, p] for p in range(4)]
-                dscores = [(e.astype(F32) * x).astype(BF16) for e, x in zip(raised, inner)]
-                dvalues = [dot_tn(e, g) for e, g in zip(raised, grads)]
-                dkeys = [dot_tn(ds, q) for ds, q in zip(dscores, queries)]
-                dqueries = [
-                    dot(ds, vm.proj[wide, 512 + pair.start : 512 + pair.stop]) for pair, ds in zip(pairs, dscores)
-                ]
-                for p, pair in enumerate(pairs):
-                    vm.dproj_f[at, pair] = (one_row(dqueries[p]) * 0.125).astype(BF16)
-                    vm.dproj_f[at, 512 + pair.start : 512 + pair.stop] = dkeys[p][:UNIT].astype(BF16)
-                    vm.dproj_f[at, 1024 + pair.start : 1024 + pair.stop] = dvalues[p][:UNIT].astype(BF16)
-
-            loop(2, fine_attend_grad)
-            grad = dot_nt(vm.dproj_f[level_at(l), :], ld.fine_qkv[...])
-            grad = norm_grad(grad, vm.hat_f[level_at(l), :], vm.scale_f[level_at(l), :1])
-            dunit = (vm.dmixed[level_at(l), :].astype(F32) + grad).astype(BF16)
-            ordered = dot(ld.to_unit_t[...], dunit).astype(BF16)
+        def fine_attend_grad(n):
+            start = base + n * UNIT
+            at, wide = rows_at(start, UNIT), rows_at(start, 128)
+            pairs = [slice(128 * p, 128 * p + 128) for p in range(4)]
+            minus = jnp.full((128, 128), -1.0, BF16)
+            grads = [two_heads(vm.dheads_f[at, pair], vm.heads2) for pair in pairs]
+            prods = [two_heads(vm.dprod_f[at, pair], vm.heads2) for pair in pairs]
+            queries = [two_heads(vm.proj[at, pair], vm.heads2) for pair in pairs]
+            inner = [
+                dot_nt(
+                    jnp.concatenate([g, d], axis=1),
+                    jnp.concatenate([vm.proj[wide, 1024 + pair.start : 1024 + pair.stop], minus], axis=1),
+                )
+                for pair, g, d in zip(pairs, grads, prods)
+            ]
+            raised = [vm.raised_f[strip * 4 + n, p] for p in range(4)]
+            dscores = [(e.astype(F32) * x).astype(BF16) for e, x in zip(raised, inner)]
+            dvalues = [dot_tn(e, g) for e, g in zip(raised, grads)]
+            dkeys = [dot_tn(ds, q) for ds, q in zip(dscores, queries)]
+            dqueries = [
+                dot(ds, vm.proj[wide, 512 + pair.start : 512 + pair.stop]) for pair, ds in zip(pairs, dscores)
+            ]
+            for p, pair in enumerate(pairs):
+                vm.dproj_f[at, pair] = (one_row(dqueries[p]) * 0.125).astype(BF16)
+                vm.dproj_f[at, 512 + pair.start : 512 + pair.stop] = dkeys[p][:UNIT].astype(BF16)
+                vm.dproj_f[at, 1024 + pair.start : 1024 + pair.stop] = dvalues[p][:UNIT].astype(BF16)
+
+        loop(4, fine_attend_grad)
+        grad = dot_nt(vm.dproj_f[both_levels, :], ld.fine_qkv[...])
+        grad = norm_grad(grad, vm.hat_f[both_levels, :], vm.scale_f[both_levels, :1])
+        dunit = (vm.dmixed[both_levels, :].astype(F32) + grad).astype(BF16)
+        for l in range(2):
+            ordered = dot(ld.to_unit_t[...], dunit[160 * l : 160 * l + 160]).astype(BF16)
             vm.send4[l, pl.ds(2 * strip, 2)] = ordered.reshape(2, QUARTER, 512)
             at_strip(strip, lambda keep: send(3, l, keep))
-
-        loop(2, fine_level_back)
 
     loop(2, fine_backward)
     by_parity(left_mask.wait_send, lambda: None)

time: 71.7 us -> 66.5 us (0.927); the launches traced: 70.5 us -> 66.1 us
  Pallas kernels: 69.9 us -> 65.4 us
    pallas_call x1, Pallas kernels: 67.9 us -> 63.5 us  [per_device(): pl.pallas_call(functools.partial(kernel, n_lat, n_lon), out_shape=(jax.Sh...]
where the time goes in v4:
time: 66.5 us; the launch traced here: 66.1 us
  Pallas kernels  65.4 us (98%)
    pallas_call x1, Pallas kernels, per_device(): pl.pallas_call(functools.partial(kernel, n_lat, n_lon), out_shape=(jax.Sh...  63.5 us
    pallas_call x1, Pallas kernels, per_device(): pl.pallas_call(hand_over, out_shape=(jax.ShapeDtypeStruct((12, 6, 2, 1024...  1.99 us

profile of v4, /device:TPU:0, one launch (start us, length us, event | category | flops | bytes accessed | tf_op | source)
XLA Modules:
  0.0 66.1 jit_solution(112643001870744822)
XLA Ops:
  0.6 63.5 %shard_map.203 = (bf16[12,6,2,1024]{3,2,1,0:T(2,128)(2,1)}, bf16[2,288,512]{2,1,0:T(8,128)(2,1)}) custom-call(bf16[2,288,512]{2,1,0:T(8,128)(2,1)} %bitcast.10, s32[12,2,24]{2,1,0:T(2,128)} %bitcast.13, f32[8,144,144]{2,1,0:T(8,128)} %refs_2_.1, bf16[512,1536]{1,0:T(8,128)(2,1)} %refs_3_.1, bf16[512,512]{1,0:T(8,128)(2,1)} %refs_4_.1, ...), custom_call_target="tpu_custom_call" | custom-call | tf_op jit(solution)/shard_map/pallas_call | solution.py:655
  64.1 2.0 %shard_map.204 = (bf16[12,6,2,1024]{3,2,1,0:T(2,128)(2,1)}, bf16[8,72,512]{2,1,0:T(8,128)(2,1)}) custom-call(bf16[12,6,2,1024]{3,2,1,0:T(2,128)(2,1)} %get-tuple-element.6.refs_0_, bf16[8,72,512]{2,1,0:T(8,128)(2,1)} %bitcast.11), custom_call_target="tpu_custom_call" | custom-call | tf_op jit(solution)/shard_map/pallas_call | solution.py:678

commit v5 on v4

--- a/solution.py
+++ b/solution.py
@@ -107,11 +107,16 @@
 
 
 def rows_at(start, size, unit=16):
-    return pl.ds(pl.multiple_of(start, unit), size)
-
-
-def loop(count, body):
-    lax.fori_loop(0, count, lambda t, c: (body(t), c)[1], 0)
+    return pl.ds(start if isinstance(start, int) else pl.multiple_of(start, unit), size)
+
+
+def loop(count, body, together=1):
+    def step(t, carry):
+        for n in range(together):
+            body(together * t + n)
+        return carry
+
+    lax.fori_loop(0, count // together, step, 0)
 
 
 class Box:
@@ -340,7 +345,8 @@
         vm.send1[l] = dot(ld.to_region[...], ld.tokens[l]).astype(BF16).reshape(4, QUARTER, 512)
         send(0, l)
 
-    loop(2, regions)
+    for l in range(2):
+        regions(l)
     partner_cot = remote(
         hbm.cotangent.at[pl.ds(6 - 6 * odd, 6)], vm.cot2.at[odd], 32, 0, device(0, 1 - 2 * odd)
     )
@@ -420,7 +426,7 @@
                 vm.recip_f[at, pair] = recip
                 vm.heads_f[at, pair] = (one_row(sums[p][:, :128]) * recip).astype(BF16)
 
-        loop(4, fine_attend)
+        loop(4, fine_attend, 2)
         mixed = vm.unit_x[both_levels, :].astype(F32) + dot(vm.heads_f[both_levels, :], ld.fine_out[...])
         mixed = mixed.astype(BF16)
         for l in range(2):
@@ -461,7 +467,8 @@
         vm.scale_m[at, :] = jnp.broadcast_to(scale, (48, 128))
         vm.normed_m[at, :] = hat.astype(BF16)
 
-    loop(3, merge_norm)
+    for t in range(3):
+        merge_norm(t)
 
     vm.merged[...] = dot(vm.normed_m[...], ld.merge_weight[...]).astype(BF16)
 
@@ -472,7 +479,8 @@
         vm.scale_c[at, :] = jnp.broadcast_to(scale, (48, 128))
         vm.normed_c[at, :] = hat.astype(BF16)
 
-    loop(3, coarse_norm)
+    for t in range(3):
+        coarse_norm(t)
 
     projected = dot(vm.normed_c[...], ld.coarse_qkv[...])
     vm.proj_c[:144, :1024] = (projected[:, :1024] * 0.125).astype(BF16)
@@ -501,7 +509,7 @@
             vm.recip_c[:, cols_at(p, 0)] = recip
             vm.heads_c[:, cols_at(p, 0)] = (one_row(total[:, :128]) * recip).astype(BF16)
 
-    loop(4, coarse_attend)
+    loop(4, coarse_attend, 2)
 
     mixed = dot(vm.heads_c[...], ld.coarse_out[...])
     vm.result[...] = (vm.merged[...].astype(F32) + mixed).astype(BF16)
@@ -534,7 +542,7 @@
             vm.dproj_c[:, cols_at(p, 0)] = (dq * 0.125).astype(BF16)
             vm.dproj_c[:, cols_at(p, 1024)] = dot_tn(ds, q)[:144].astype(BF16)
 
-    loop(4, coarse_attend_grad)
+    loop(4, coarse_attend_grad, 2)
 
     vm.grad_c[...] = dot_nt(vm.dproj_c[...], ld.coarse_qkv[...])
 
@@ -543,7 +551,8 @@
         grad = norm_grad(vm.grad_c[at, :], vm.hat_c[at, :], vm.scale_c[at, :1])
         vm.dmerged[at, :] = (vm.cot[at, :].astype(F32) + grad).astype(BF16)
 
-    loop(3, coarse_norm_grad)
+    for t in range(3):
+        coarse_norm_grad(t)
 
     vm.grad_m[...] = dot_nt(vm.dmerged[...], ld.merge_weight[...])
     loads.merge_t.wait()
@@ -598,7 +607,7 @@
                 vm.dproj_f[at, 512 + pair.start : 512 + pair.stop] = dkeys[p][:UNIT].astype(BF16)
                 vm.dproj_f[at, 1024 + pair.start : 1024 + pair.stop] = dvalues[p][:UNIT].astype(BF16)
 
-        loop(4, fine_attend_grad)
+        loop(4, fine_attend_grad, 2)
         grad = dot_nt(vm.dproj_f[both_levels, :], ld.fine_qkv[...])
         grad = norm_grad(grad, vm.hat_f[both_levels, :], vm.scale_f[both_levels, :1])
         dunit = (vm.dmixed[both_levels, :].astype(F32) + grad).astype(BF16)

time: 66.5 us -> 63.6 us (0.956)
  Pallas kernels: 65.4 us -> 62.5 us
    pallas_call x1, Pallas kernels: 63.5 us -> 60.5 us  [per_device(): pl.pallas_call(functools.partial(kernel, n_lat, n_lon), out_shape=(jax.Sh...]
where the time goes in v5:
time: 63.6 us; the launch traced here: 63.3 us
  Pallas kernels  62.5 us (98%)
  between operations  0.8 us (1%)
    pallas_call x1, Pallas kernels, per_device(): pl.pallas_call(functools.partial(kernel, n_lat, n_lon), out_shape=(jax.Sh...  60.5 us
    pallas_call x1, Pallas kernels, per_device(): pl.pallas_call(hand_over, out_shape=(jax.ShapeDtypeStruct((12, 6, 2, 1024...  1.99 us

profile of v5, /device:TPU:0, one launch (start us, length us, event | category | flops | bytes accessed | tf_op | source)
XLA Modules:
  0.0 63.3 jit_solution(4829813747556494325)
XLA Ops:
  0.6 60.5 %shard_map.203 = (bf16[12,6,2,1024]{3,2,1,0:T(2,128)(2,1)}, bf16[2,288,512]{2,1,0:T(8,128)(2,1)}) custom-call(bf16[2,288,512]{2,1,0:T(8,128)(2,1)} %bitcast.10, s32[12,2,24]{2,1,0:T(2,128)} %bitcast.13, f32[8,144,144]{2,1,0:T(8,128)} %refs_2_.1, bf16[512,1536]{1,0:T(8,128)(2,1)} %refs_3_.1, bf16[512,512]{1,0:T(8,128)(2,1)} %refs_4_.1, ...), custom_call_target="tpu_custom_call" | custom-call | tf_op jit(solution)/shard_map/pallas_call | solution.py:664
  61.1 2.0 %shard_map.204 = (bf16[12,6,2,1024]{3,2,1,0:T(2,128)(2,1)}, bf16[8,72,512]{2,1,0:T(8,128)(2,1)}) custom-call(bf16[12,6,2,1024]{3,2,1,0:T(2,128)(2,1)} %get-tuple-element.6.refs_0_, bf16[8,72,512]{2,1,0:T(8,128)(2,1)} %bitcast.11), custom_call_target="tpu_custom_call" | custom-call | tf_op jit(solution)/shard_map/pallas_call | solution.py:687

commit v6 on v5

--- a/solution.py
+++ b/solution.py
@@ -426,13 +426,15 @@
                 vm.recip_f[at, pair] = recip
                 vm.heads_f[at, pair] = (one_row(sums[p][:, :128]) * recip).astype(BF16)
 
-        loop(4, fine_attend, 2)
-        mixed = vm.unit_x[both_levels, :].astype(F32) + dot(vm.heads_f[both_levels, :], ld.fine_out[...])
-        mixed = mixed.astype(BF16)
-        for l in range(2):
-            ordered = dot(ld.to_unit_t[...], mixed[160 * l : 160 * l + 160]).astype(BF16)
+        def fine_level(l):
+            for m in range(2):
+                fine_attend(2 * l + m)
+            mixed = vm.unit_x[level_at(l), :].astype(F32) + dot(vm.heads_f[level_at(l), :], ld.fine_out[...])
+            ordered = dot(ld.to_unit_t[...], mixed.astype(BF16)).astype(BF16)
             vm.send2[l, pl.ds(2 * strip, 2)] = ordered.reshape(2, QUARTER, 512)
             at_strip(strip, lambda keep: send(1, l, keep))
+
+        loop(2, fine_level)
 
     loop(2, fine_forward)
     loads.coarse_bias.wait()
@@ -607,14 +609,17 @@
                 vm.dproj_f[at, 512 + pair.start : 512 + pair.stop] = dkeys[p][:UNIT].astype(BF16)
                 vm.dproj_f[at, 1024 + pair.start : 1024 + pair.stop] = dvalues[p][:UNIT].astype(BF16)
 
-        loop(4, fine_attend_grad, 2)
-        grad = dot_nt(vm.dproj_f[both_levels, :], ld.fine_qkv[...])
-        grad = norm_grad(grad, vm.hat_f[both_levels, :], vm.scale_f[both_levels, :1])
-        dunit = (vm.dmixed[both_levels, :].astype(F32) + grad).astype(BF16)
-        for l in range(2):
-            ordered = dot(ld.to_unit_t[...], dunit[160 * l : 160 * l + 160]).astype(BF16)
+        def fine_level_back(l):
+            for m in range(2):
+                fine_attend_grad(2 * l + m)
+            grad = dot_nt(vm.dproj_f[level_at(l), :], ld.fine_qkv[...])
+            grad = norm_grad(grad, vm.hat_f[level_at(l), :], vm.scale_f[level_at(l), :1])
+            dunit = (vm.dmixed[level_at(l), :].astype(F32) + grad).astype(BF16)
+            ordered = dot(ld.to_unit_t[...], dunit).astype(BF16)
             vm.send4[l, pl.ds(2 * strip, 2)] = ordered.reshape(2, QUARTER, 512)
             at_strip(strip, lambda keep: send(3, l, keep))
+
+        loop(2, fine_level_back)
 
     loop(2, fine_backward)
     by_parity(left_mask.wait_send, lambda: None)

time: 63.6 us -> 63.9 us (level); the launches traced: 63.3 us -> 62.8 us
  no operation moved by 1% of the time
where the time goes in v6:
time: 63.9 us; the launch traced here: 62.8 us
  Pallas kernels  62.2 us (97%)
  between operations  0.64 us (1%)
    pallas_call x1, Pallas kernels, per_device(): pl.pallas_call(functools.partial(kernel, n_lat, n_lon), out_shape=(jax.Sh...  60.2 us
    pallas_call x1, Pallas kernels, per_device(): pl.pallas_call(hand_over, out_shape=(jax.ShapeDtypeStruct((12, 6, 2, 1024...  1.99 us

profile of v6, /device:TPU:0, one launch (start us, length us, event | category | flops | bytes accessed | tf_op | source)
XLA Modules:
  0.0 62.8 jit_solution(4226957302941003601)
XLA Ops:
  0.6 60.2 %shard_map.203 = (bf16[12,6,2,1024]{3,2,1,0:T(2,128)(2,1)}, bf16[2,288,512]{2,1,0:T(8,128)(2,1)}) custom-call(bf16[2,288,512]{2,1,0:T(8,128)(2,1)} %bitcast.10, s32[12,2,24]{2,1,0:T(2,128)} %bitcast.13, f32[8,144,144]{2,1,0:T(8,128)} %refs_2_.1, bf16[512,1536]{1,0:T(8,128)(2,1)} %refs_3_.1, bf16[512,512]{1,0:T(8,128)(2,1)} %refs_4_.1, ...), custom_call_target="tpu_custom_call" | custom-call | tf_op jit(solution)/shard_map/pallas_call | solution.py:669
  60.9 2.0 %shard_map.204 = (bf16[12,6,2,1024]{3,2,1,0:T(2,128)(2,1)}, bf16[8,72,512]{2,1,0:T(8,128)(2,1)}) custom-call(bf16[12,6,2,1024]{3,2,1,0:T(2,128)(2,1)} %get-tuple-element.6.refs_0_, bf16[8,72,512]{2,1,0:T(8,128)(2,1)} %bitcast.11), custom_call_target="tpu_custom_call" | custom-call | tf_op jit(solution)/shard_map/pallas_call | solution.py:692

commit v7 on v5

--- a/solution.py
+++ b/solution.py
@@ -426,13 +426,15 @@
                 vm.recip_f[at, pair] = recip
                 vm.heads_f[at, pair] = (one_row(sums[p][:, :128]) * recip).astype(BF16)
 
-        loop(4, fine_attend, 2)
-        mixed = vm.unit_x[both_levels, :].astype(F32) + dot(vm.heads_f[both_levels, :], ld.fine_out[...])
-        mixed = mixed.astype(BF16)
-        for l in range(2):
-            ordered = dot(ld.to_unit_t[...], mixed[160 * l : 160 * l + 160]).astype(BF16)
+        def fine_level(l):
+            for m in range(2):
+                fine_attend(2 * l + m)
+            mixed = vm.unit_x[level_at(l), :].astype(F32) + dot(vm.heads_f[level_at(l), :], ld.fine_out[...])
+            ordered = dot(ld.to_unit_t[...], mixed.astype(BF16)).astype(BF16)
             vm.send2[l, pl.ds(2 * strip, 2)] = ordered.reshape(2, QUARTER, 512)
             at_strip(strip, lambda keep: send(1, l, keep))
+
+        loop(2, fine_level)
 
     loop(2, fine_forward)
     loads.coarse_bias.wait()

time: 63.6 us -> 63.2 us (level)
  Pallas kernels: 62.5 us -> 61.7 us
    pallas_call x1, Pallas kernels: 60.5 us -> 59.7 us  [per_device(): pl.pallas_call(functools.partial(kernel, n_lat, n_lon), out_shape=(jax.Sh...]
where the time goes in v7:
time: 63.2 us; the launch traced here: 62.5 us
  Pallas kernels  61.7 us (98%)
  between operations  0.8 us (1%)
    pallas_call x1, Pallas kernels, per_device(): pl.pallas_call(functools.partial(kernel, n_lat, n_lon), out_shape=(jax.Sh...  59.7 us
    pallas_call x1, Pallas kernels, per_device(): pl.pallas_call(hand_over, out_shape=(jax.ShapeDtypeStruct((12, 6, 2, 1024...  1.99 us

profile of v7, /device:TPU:0, one launch (start us, length us, event | category | flops | bytes accessed | tf_op | source)
XLA Modules:
  0.0 62.5 jit_solution(3478564854255015376)
XLA Ops:
  0.6 59.7 %shard_map.203 = (bf16[12,6,2,1024]{3,2,1,0:T(2,128)(2,1)}, bf16[2,288,512]{2,1,0:T(8,128)(2,1)}) custom-call(bf16[2,288,512]{2,1,0:T(8,128)(2,1)} %bitcast.10, s32[12,2,24]{2,1,0:T(2,128)} %bitcast.13, f32[8,144,144]{2,1,0:T(8,128)} %refs_2_.1, bf16[512,1536]{1,0:T(8,128)(2,1)} %refs_3_.1, bf16[512,512]{1,0:T(8,128)(2,1)} %refs_4_.1, ...), custom_call_target="tpu_custom_call" | custom-call | tf_op jit(solution)/shard_map/pallas_call | solution.py:666
  60.4 2.0 %shard_map.204 = (bf16[12,6,2,1024]{3,2,1,0:T(2,128)(2,1)}, bf16[8,72,512]{2,1,0:T(8,128)(2,1)}) custom-call(bf16[12,6,2,1024]{3,2,1,0:T(2,128)(2,1)} %get-tuple-element.6.refs_0_, bf16[8,72,512]{2,1,0:T(8,128)(2,1)} %bitcast.11), custom_call_target="tpu_custom_call" | custom-call | tf_op jit(solution)/shard_map/pallas_call | solution.py:689
